TPU v7x, 32 devices: a whole 2x2x4 slice. The times are simulated.
32 devices in a mesh: groups: 2 (over y), dp: 4 (over x, core), tensor: 4 (over z).
Axes of the slice: x: 2, y: 2, z: 4, core: 2. Of those that a mesh axis runs over, the one named last changes fastest.
Arguments:
- gate_pre: bfloat16 [2048, 16384], P(('groups', 'dp'), 'tensor'), parts along dimension 0, may hold values from -6 to 6
- up_pre: bfloat16 [2048, 16384], P(('groups', 'dp'), 'tensor'), parts along dimension 0, may hold values from -6 to 6
- down_weight: bfloat16 [16384, 4096], P('tensor', 'dp'), may hold values from -0.0625 to 0.0625
- block_mask: int32 [128, 32], P('tensor'), may hold values from 0 to 1, as said below
- grad_out: bfloat16 [2048, 4096], P(('groups', 'dp'), 'tensor'), parts along dimension 0, may hold values from -6 to 6
Outputs:
- output: bfloat16 [2048, 4096], P(('groups', 'dp'), 'tensor'), parts along dimension 0
- d_gate: bfloat16 [2048, 16384], P(('groups', 'dp'), 'tensor'), parts along dimension 0
- d_up: bfloat16 [2048, 16384], P(('groups', 'dp'), 'tensor'), parts along dimension 0
- d_weight: float32 [32768, 4096], P(('groups', 'tensor'), 'dp'), parts along dimension 0
There are 2 independent parts, one for each index of `groups`. A program takes and returns all parts, laid end to end along the dimension named above; an argument that names none is the same for every part. Nothing has to cross between parts.
Inputs may be any that keep to these rules, and one draw needn't show every extreme that they name: block_mask holds 0 and 1. In each device's shard of down_weight (32 block rows of one tensor index by 8 block columns of one dp index) between 96 and 160 blocks are kept; all shards of some tensor index keep exactly 160.
All inputs are finite; a program needn't handle non-finite values.
Results may differ from a plain program's by a relative error of at most 0.0051.
Values may be sent and summed in bfloat16 or wider, within the bound.
No kernel may reach another device: no remote copies, remote signals or barrier semaphores. Data moves between devices by JAX's collectives and lax.ppermute only.
A program may use at most 192 MiB of HBM per device.

v0:
```python
import jax
import jax.numpy as jnp
from jax import lax
from jax.sharding import PartitionSpec as P

BLK = 128


def expand_mask(small_mask):
    widened = jnp.repeat(jnp.repeat(small_mask, BLK, axis=0), BLK, axis=1)
    return widened


def per_device(gate_pre, up_pre, down_weight, block_mask, grad_out):
    d_local = down_weight.shape[1]
    d_blocks = d_local // BLK
    own_mask = lax.dynamic_slice_in_dim(block_mask, lax.axis_index("dp") * d_blocks, d_blocks, 1)
    keep_wide = expand_mask(own_mask)
    masked = down_weight * keep_wide.astype(jnp.bfloat16)
    gate_val = gate_pre.astype(jnp.float32)
    up_val = up_pre.astype(jnp.float32)
    gate_sig = jax.nn.sigmoid(gate_val)
    active = gate_val * gate_sig
    hidden = (active * up_val).astype(jnp.bfloat16)
    full_grad = lax.all_gather(grad_out, "tensor", axis=1, tiled=True)
    gathered = lax.all_gather(masked, "dp", axis=1, tiled=True)
    d_hidden = lax.dot_general(
        full_grad, gathered, (((1,), (1,)), ((), ())), preferred_element_type=jnp.float32
    )
    output = lax.psum_scatter(
        jnp.dot(hidden, gathered, preferred_element_type=jnp.float32),
        "tensor",
        scatter_dimension=1,
        tiled=True,
    ).astype(jnp.bfloat16)
    d_gate = (d_hidden * up_val * gate_sig * (1.0 + gate_val * (1.0 - gate_sig))).astype(
        jnp.bfloat16
    )
    d_up = (d_hidden * active).astype(jnp.bfloat16)
    grad_cols = lax.all_to_all(full_grad, "dp", split_axis=1, concat_axis=0, tiled=True)
    d_weight = lax.dot_general(
        lax.all_gather(hidden, "dp", axis=0, tiled=True),
        grad_cols,
        (((0,), (0,)), ((), ())),
        preferred_element_type=jnp.float32,
    )
    d_weight = d_weight * keep_wide.astype(jnp.float32)
    return (output, d_gate, d_up, d_weight)


def solution(mesh):
    return jax.shard_map(
        per_device,
        mesh=mesh,
        in_specs=(
            P(("groups", "dp"), "tensor"),
            P(("groups", "dp"), "tensor"),
            P("tensor", "dp"),
            P("tensor", None),
            P(("groups", "dp"), "tensor"),
        ),
        out_specs=(
            P(("groups", "dp"), "tensor"),
            P(("groups", "dp"), "tensor"),
            P(("groups", "dp"), "tensor"),
            P(("groups", "tensor"), "dp"),
        ),
        check_vma=False,
    )
```

profile of v0, /device:TPU:0, one launch (start us, length us, event | category | flops | bytes accessed | tf_op | source)
XLA Modules:
  0.0 473.2 jit_solution(6119169817881139850)
XLA Ops:
  7.2 0.0 all-gather.6.cloned.1.call-start
  7.2 2.0 copy.19
  9.3 0.0 all-gather.6.cloned.1.call-update
  9.3 0.0 all-gather.4.cloned.1.call-start
  9.3 0.8 dynamic-slice_convert_fusion
  10.1 0.1 broadcast_in_dim.10
  10.3 0.0 copy-start.1
  10.3 11.7 %broadcast_in_dim.11 = bf16[4096,8,128]{2,1,0:T(8,128)(2,1)S(1)} broadcast(bf16[4096,8]{1,0:T(8,128)(2,1)S(1)} %bitcast.23), dimensions={0,1} | broadcast | bytes 8454144 | tf_op jit(solution)/shard_map/broadcast_in_dim | solution.py:10
  22.0 4.0 bitcast_multiply_fusion.1
  26.0 0.0 all-gather.4.cloned.1.call-update
  26.1 0.0 reduce-scatter.2.cloned.1.call-start
  26.1 1.5 copy-done.2
  27.6 2.4 copy.17
  30.1 4.1 copy.18
  34.1 24.7 %all-gather.6.cloned.1.call-done = bf16[256,4096]{0,1:T(8,128)(2,1)} async-done(((bf16[256,1024]{0,1:T(8,128)(2,1)}), bf16[256,4096]{0,1:T(8,128)(2,1)}) %all-gather.6.cloned.1.call-update) | async-done | bytes 2097168 | tf_op jit(solution)/shard_map/all_gather | solution.py:25
  58.8 202.4 %all-gather.4.cloned.1.call-done = bf16[4096,4096]{1,0:T(8,128)(2,1)} async-done(((bf16[4096,1024]{1,0:T(8,128)(2,1)}), bf16[4096,4096]{1,0:T(8,128)(2,1)}) %all-gather.4.cloned.1.call-update) | async-done | bytes 33554448 | tf_op jit(solution)/shard_map/all_gather | solution.py:26
  261.2 20.0 %multiply_convert_fusion = (bf16[256,4096]{0,1:T(8,128)(2,1)}, bf16[256,4096]{0,1:T(8,128)(2,1)}, bf16[256,4096]{0,1:T(8,128)(2,1)S(1)}) fusion(bf16[256,4096]{0,1:T(8,128)(2,1)} %copy.17, bf16[256,4096]{0,1:T(8,128)(2,1)} %copy.18, bf16[4096,4096]{1,0:T(8,128)(2,1)} %all-gather.4.cloned.1.call-done, bf16[256,4096]{0,1:T(8,128)(2,1)} %all-gather.6.cloned.1.call-done), kind=kOutput, calls=%fused_computation.16 | convolution fusion | flops 8607760384 | bytes 46137344 | tf_op jit(solution)/shard_map/dot_general | solution.py:27
  281.2 17.9 %fusion.8 = f32[256,4096]{1,0:T(8,128)} fusion(bf16[256,4096]{0,1:T(8,128)(2,1)S(1)} %get-tuple-element.18, bf16[4096,4096]{1,0:T(8,128)(2,1)} %all-gather.4.cloned.1.call-done), kind=kOutput, calls=%fused_computation.19 | convolution fusion | flops 8589934592 | bytes 39845888 | tf_op jit(solution)/shard_map/dot_general | solution.py:31
  299.1 0.0 reduce-scatter.2.cloned.1.call-update
  299.1 0.0 all-gather.8.cloned.1.call-start
  299.2 0.5 all-gather.8.cloned.1.call-update
  299.7 29.3 %all_to_all.19 = bf16[256,4,1024]{0,2,1:T(8,128)(2,1)S(1)} all-to-all(bf16[256,4,1024]{0,2,1:T(8,128)(2,1)} %bitcast.24), channel_id=1, replica_groups=mesh['groups'=2,'dp'=4,'tensor'=4] {'dp'}, dimensions={1} | all-to-all | bytes 4194304 | tf_op jit(solution)/shard_map/all_to_all | solution.py:40
  329.0 2.4 copy.20
  331.4 4.2 copy.21
  335.7 2.8 copy.22
  338.5 37.5 %reduce-scatter.2.cloned.1.call-done = f32[256,1024]{1,0:T(8,128)} async-done(((f32[256,4096]{1,0:T(8,128)}), f32[256,1024]{1,0:T(8,128)}) %reduce-scatter.2.cloned.1.call-update) | async-done | bytes 1048592 | tf_op jit(solution)/shard_map/reduce_scatter | solution.py:30
  376.1 2.1 convert_element_type.46
  378.2 59.3 %all-gather.8.cloned.1.call-done = bf16[1024,4096]{0,1:T(8,128)(2,1)} async-done(((bf16[256,4096]{0,1:T(8,128)(2,1)}), bf16[1024,4096]{0,1:T(8,128)(2,1)}) %all-gather.8.cloned.1.call-update) | async-done | bytes 8388624 | tf_op jit(solution)/shard_map/all_gather | solution.py:42
  437.5 0.1 broadcast_in_dim.12
  437.6 0.0 slice-start.1
  437.6 10.7 %broadcast_in_dim.13 = f32[4096,8,128]{2,1,0:T(8,128)} broadcast(f32[4096,8]{1,0:T(8,128)S(1)} %bitcast.21), dimensions={0,1} | broadcast | bytes 16908288 | tf_op jit(solution)/shard_map/broadcast_in_dim | solution.py:10
  448.3 18.4 %bitcast_multiply_fusion = f32[4096,1024]{1,0:T(8,128)} fusion(f32[512,8,8,128]{3,2,1,0:T(8,128)} %bitcast.20, bf16[1024,4096]{0,1:T(8,128)(2,1)S(1)} %bitcast.27, bf16[1024,1024]{1,0:T(8,128)(2,1)S(1)} %bitcast.25), kind=kOutput, calls=%fused_computation | convolution fusion | flops 8594128896 | bytes 44040192 | tf_op jit(solution)/shard_map/dot_general | solution.py:41
  (12 shorter events, 0.0 us)
Async XLA Ops:
  7.2 51.7 %all-gather.6.cloned.1.call-start = ((), (), s32[]{:S(2)}) async-start(), calls=%async_computation.4 | async-start | bytes 2621440 | tf_op jit(solution)/shard_map/all_gather | solution.py:25
  9.3 252.0 %all-gather.4.cloned.1.call-start = ((), (), s32[]{:S(2)}) async-start(), calls=%async_computation.2 | async-start | bytes 41943040 | tf_op jit(solution)/shard_map/all_gather | solution.py:26
  10.3 11.8 %copy-start.1 = (bf16[4096,1024]{1,0:T(8,128)(2,1)S(1)}, bf16[4096,1024]{1,0:T(8,128)(2,1)}, u32[]{:S(2)}) copy-start(bf16[4096,1024]{1,0:T(8,128)(2,1)} %param.7) | copy-start | bytes 25165828
  26.0 1.6 copy-start.2
  26.1 350.0 %reduce-scatter.2.cloned.1.call-start = ((), (), s32[]{:S(2)}) async-start(), calls=%async_computation.3 | async-start | bytes 5242880 | tf_op jit(solution)/shard_map/reduce_scatter | solution.py:30
  281.2 17.9 %copy-start = (bf16[256,4096]{0,1:T(8,128)(2,1)}, bf16[256,4096]{0,1:T(8,128)(2,1)S(1)}, u32[]{:S(2)}) copy-start(bf16[256,4096]{0,1:T(8,128)(2,1)S(1)} %get-tuple-element.18) | copy-start | bytes 6291460
  299.1 138.3 %all-gather.8.cloned.1.call-start = ((), (), s32[]{:S(2)}) async-start(), calls=%async_computation.5 | async-start | bytes 10485760 | tf_op jit(solution)/shard_map/all_gather | solution.py:42
  331.4 4.2 copy-start.3
  437.5 10.8 %slice-start = ((s8[8388608]{0:T(1024)(128)(4,1)}), s8[4194304]{0:T(1024)(128)(4,1)S(1)}, s32[]{:S(2)}) async-start(s8[8388608]{0:T(1024)(128)(4,1)} %bitcast.26), calls=%async_computation.6 | async-start | bytes 8388608
  437.6 10.7 %copy-start.4 = (bf16[4,256,1024]{2,1,0:T(8,128)(2,1)S(1)}, bf16[4,256,1024]{2,1,0:T(8,128)(2,1)}, u32[]{:S(2)}) copy-start(bf16[4,256,1024]{2,1,0:T(8,128)(2,1)} %copy.20) | copy-start | bytes 6291460
  437.6 10.7 %slice-start.1 = ((s8[8388608]{0:T(1024)(128)(4,1)}), s8[4194304]{0:T(1024)(128)(4,1)S(1)}, s32[]{:S(2)}) async-start(s8[8388608]{0:T(1024)(128)(4,1)} %bitcast.26), calls=%async_computation.7 | async-start | bytes 8388608
Sparse Core Ops, SparseCore 0:
  10.1 48.6 all-gather.5
  61.0 200.2 all-gather.3
  299.3 76.7 reduce-scatter.1
  377.5 59.8 all-gather.7
where the time goes:
time: 474 us; the launch traced here: 473 us
  waiting for transfers between devices  325 us (69%)
  matrix products  56.3 us (12%)
  local copies, waits for them, and re-layouts  42.3 us (9%)
  blocking collectives  29.3 us (6%)
  between operations  13.8 us (3%)
  other arithmetic  6.87 us (1%)
    all_gather x1, waiting for transfers between devices, per_device(): gathered = lax.all_gather(masked, 'dp', axis=1, tiled=True)  202 us
    all_gather x1, waiting for transfers between devices, per_device(): lax.all_gather(hidden, 'dp', axis=0, tiled=True)  59.3 us
    reduce_scatter x1, waiting for transfers between devices, per_device(): lax.psum_scatter(jnp.dot(hidden, gathered, preferred_element_type=jnp.flo...  37.5 us
    all_to_all x1, blocking collectives, per_device(): lax.all_to_all(full_grad, 'dp', split_axis=1, concat_axis=0, tiled=True)  29.3 us
    all_gather x1, waiting for transfers between devices, per_device(): full_grad = lax.all_gather(grad_out, 'tensor', axis=1, tiled=True)  24.7 us
    broadcast_in_dim x4, local copies, waits for them, and re-layouts, expand_mask(): widened = jnp.repeat(jnp.repeat(small_mask, BLK, axis=0), BLK, axis=1)  22.7 us
    dot_general x1, matrix products, per_device(): lax.dot_general(full_grad, gathered, (((1,), (1,)), ((), ())), preferred_...  20 us
    dot_general x1, matrix products, per_device(): lax.dot_general(lax.all_gather(hidden, 'dp', axis=0, tiled=True), grad_co...  18.4 us
  transfers between devices with their start and end apart: 4, of which 4 were waited for; matrix products, arithmetic and copies ran while one was open for 7% of the time, Pallas kernels for 0%

commit v1 on v0

v1 whole, which is shorter than its diff:
```python
import functools

import jax
import jax.numpy as jnp
from jax import lax
from jax.experimental import pallas as pl
from jax.experimental.pallas import tpu as pltpu
from jax.sharding import PartitionSpec as P

BLK = 128
BF = jnp.bfloat16
F32 = jnp.float32
ROWS_CONTRACT = (((0,), (0,)), ((), ()))
COLS_CONTRACT = (((1,), (1,)), ((), ()))


def expand_mask(small_mask):
    widened = jnp.repeat(jnp.repeat(small_mask, BLK, axis=0), BLK, axis=1)
    return widened


def any_mesh(gate_pre, up_pre, down_weight, block_mask, grad_out):
    d_local = down_weight.shape[1]
    d_blocks = d_local // BLK
    own_mask = lax.dynamic_slice_in_dim(block_mask, lax.axis_index("dp") * d_blocks, d_blocks, 1)
    keep_wide = expand_mask(own_mask)
    masked = down_weight * keep_wide.astype(BF)
    gate_val = gate_pre.astype(F32)
    up_val = up_pre.astype(F32)
    gate_sig = jax.nn.sigmoid(gate_val)
    active = gate_val * gate_sig
    hidden = (active * up_val).astype(BF)
    full_grad = lax.all_gather(grad_out, "tensor", axis=1, tiled=True)
    gathered = lax.all_gather(masked, "dp", axis=1, tiled=True)
    d_hidden = lax.dot_general(full_grad, gathered, COLS_CONTRACT, preferred_element_type=F32)
    output = lax.psum_scatter(
        jnp.dot(hidden, gathered, preferred_element_type=F32),
        "tensor",
        scatter_dimension=1,
        tiled=True,
    ).astype(BF)
    d_gate = (d_hidden * up_val * gate_sig * (1.0 + gate_val * (1.0 - gate_sig))).astype(BF)
    d_up = (d_hidden * active).astype(BF)
    grad_cols = lax.all_to_all(full_grad, "dp", split_axis=1, concat_axis=0, tiled=True)
    d_weight = lax.dot_general(
        lax.all_gather(hidden, "dp", axis=0, tiled=True),
        grad_cols,
        ROWS_CONTRACT,
        preferred_element_type=F32,
    )
    d_weight = d_weight * keep_wide.astype(F32)
    return (output, d_gate, d_up, d_weight)


def mask_body(info, own, other, out):
    i = pl.program_id(0)
    half = own.shape[1]
    blocks = half // BLK
    row_blocks = own.shape[0] // BLK
    own_is_near = info[info.shape[0] - 1, 0]

    def put(src, first):
        for r in range(row_blocks):
            for k in range(blocks):
                keep = info[i * row_blocks + r, first + k].astype(F32)
                block = src[r * BLK : (r + 1) * BLK, k * BLK : (k + 1) * BLK]
                col = (first + k) * BLK
                out[r * BLK : (r + 1) * BLK, col : col + BLK] = (block.astype(F32) * keep).astype(BF)

    @pl.when(own_is_near == 1)
    def _():
        put(own, 0)
        put(other, blocks)

    @pl.when(own_is_near == 0)
    def _():
        put(other, 0)
        put(own, blocks)


def masked_pair(info, own, other):
    rows, half = own.shape
    step = 256
    return pl.pallas_call(
        mask_body,
        out_shape=jax.ShapeDtypeStruct((rows, 2 * half), BF),
        grid_spec=pltpu.PrefetchScalarGridSpec(
            num_scalar_prefetch=1,
            grid=(rows // step,),
            in_specs=[
                pl.BlockSpec((step, half), lambda i, _: (i, 0)),
                pl.BlockSpec((step, half), lambda i, _: (i, 0)),
            ],
            out_specs=pl.BlockSpec((step, 2 * half), lambda i, _: (i, 0)),
        ),
        compiler_params=pltpu.CompilerParams(vmem_limit_bytes=32 * 2**20),
        name="masked_pair",
    )(info, own, other)


def dw_body(n, keep_ref, *refs):
    hid, grads, out = refs[:n], refs[n : 2 * n], refs[2 * n]
    i = pl.program_id(0)
    total = None
    for h, g in zip(hid, grads):
        part = lax.dot_general(h[...], g[...], ROWS_CONTRACT, preferred_element_type=F32)
        total = part if total is None else total + part
    for r in range(out.shape[0] // BLK):
        for k in range(out.shape[1] // BLK):
            keep = keep_ref[i * (out.shape[0] // BLK) + r, k].astype(F32)
            rows, cols = slice(r * BLK, (r + 1) * BLK), slice(k * BLK, (k + 1) * BLK)
            out[rows, cols] = total[rows, cols] * keep


def weight_grad(keep, hidden, grads):
    n = len(hidden)
    hid_all = hidden[0].shape[1]
    cols = grads[0].shape[1]
    step = 512
    return pl.pallas_call(
        functools.partial(dw_body, n),
        out_shape=jax.ShapeDtypeStruct((hid_all, cols), F32),
        grid_spec=pltpu.PrefetchScalarGridSpec(
            num_scalar_prefetch=1,
            grid=(hid_all // step,),
            in_specs=[pl.BlockSpec((h.shape[0], step), lambda i, _: (0, i)) for h in hidden]
            + [pl.BlockSpec(g.shape, lambda i, _: (0, 0)) for g in grads],
            out_specs=pl.BlockSpec((step, cols), lambda i, _: (i, 0)),
        ),
        compiler_params=pltpu.CompilerParams(vmem_limit_bytes=48 * 2**20),
        name="weight_grad",
    )(keep, *hidden, *grads)


def four_by_four(gate_pre, up_pre, down_weight, block_mask, grad_out):
    n_dp = n_t = 4
    d, z = lax.axis_index("dp"), lax.axis_index("tensor")
    x, c = d // 2, d % 2
    q = jnp.where(x == 0, z, n_t - 1 - z)
    near = 2 * x + (1 - x)
    far = 2 * x + x
    own_near = d == near
    tokens, hid = gate_pre.shape
    cols = down_weight.shape[1]
    d_blocks = cols // BLK

    def place(dd, qq):
        return dd * n_t + (qq if dd // 2 == 0 else n_t - 1 - qq)

    def hop(a, *pairs):
        perm = [(place(dd, s), place(dd, t)) for dd in range(n_dp) for s, t in pairs]
        return lax.ppermute(a, ("dp", "tensor"), perm)

    def over_x(a):
        return lax.ppermute(a, "dp", [(i, i ^ 2) for i in range(n_dp)])

    def over_core(a):
        return lax.ppermute(a, "dp", [(i, i ^ 1) for i in range(n_dp)])

    roots = [(dd, qq) for dd in range(n_dp) for qq in (0, 1)]

    def to_roots(a):
        perm = [((dd ^ 2) * n_t + place(dd, qq) % n_t, place(dd, qq)) for dd, qq in roots]
        return lax.ppermute(a, ("dp", "tensor"), perm)

    def from_roots(a):
        perm = [(place(dd, qq), (dd ^ 2) * n_t + place(dd, qq) % n_t) for dd, qq in roots]
        return lax.ppermute(a, ("dp", "tensor"), perm)

    def pass_along(g):
        r1 = hop(g, (0, 1), (1, 2))
        dn = hop(g, (1, 0))
        r2 = hop(r1, (1, 2), (2, 3))
        r3 = hop(r2, (2, 3))
        g_near = jnp.where(q == 0, dn, jnp.where(q == 1, g, jnp.where(q == 2, r1, r2)))
        g_far = jnp.where(q == 0, g, jnp.where(q == 1, r1, jnp.where(q == 2, r2, r3)))
        return g_near, g_far

    grad_x = to_roots(grad_out)
    near1, far1 = pass_along(grad_x)
    near0, far0 = pass_along(grad_out)

    gate_val = gate_pre.astype(F32)
    up_val = up_pre.astype(F32)
    gate_sig = jax.nn.sigmoid(gate_val)
    active = gate_val * gate_sig
    hidden0 = (active * up_val).astype(BF)
    half = tokens // 2
    hidden1 = [over_x(hidden0[i * half : (i + 1) * half]) for i in range(2)]

    other = over_core(down_weight)
    keep_near = lax.dynamic_slice_in_dim(block_mask, near * d_blocks, d_blocks, 1)
    keep_far = lax.dynamic_slice_in_dim(block_mask, far * d_blocks, d_blocks, 1)
    keep_own = lax.dynamic_slice_in_dim(block_mask, d * d_blocks, d_blocks, 1)
    flag = jnp.full((1, 2 * d_blocks), own_near, jnp.int32)
    info = jnp.concatenate([jnp.concatenate([keep_near, keep_far], 1), flag], 0)
    pair = masked_pair(info, down_weight, other)

    def reduced(h):
        o = jnp.dot(h, pair, preferred_element_type=F32)
        o_near, o_far = o[:, :cols], o[:, cols:]
        e1 = hop(o_far.astype(BF), (3, 2))
        e2 = hop(o_near.astype(BF), (3, 2), (0, 1))
        e3 = hop((o_far + e1.astype(F32)).astype(BF), (2, 1))
        o_near = o_near + e2.astype(F32)
        e4 = hop(o_near.astype(BF), (2, 1))
        e5 = hop((o_far + e3.astype(F32)).astype(BF), (1, 0))
        return jnp.where(q == 0, o_far + e5.astype(F32), o_near + e4.astype(F32)).astype(BF)

    out1 = [from_roots(reduced(h)) for h in hidden1]
    out0 = reduced(hidden0)
    output = jnp.where(q < 2, out0, jnp.concatenate(out1, 0))

    both1 = jnp.concatenate([near1, far1], 1)
    both0 = jnp.concatenate([near0, far0], 1)
    n_chunk = 4
    width = hid // n_chunk
    d_gate, d_up = [], []
    for k in range(n_chunk):
        s = slice(k * width, (k + 1) * width)
        w = pair[s]
        sent = lax.dot_general(both1, w, COLS_CONTRACT, preferred_element_type=F32).astype(BF)
        got = over_x(sent)
        d_hidden = lax.dot_general(both0, w, COLS_CONTRACT, preferred_element_type=F32)
        d_hidden = d_hidden + got.astype(F32)
        gv, uv, sg = gate_val[:, s], up_val[:, s], gate_sig[:, s]
        d_gate.append((d_hidden * uv * sg * (1.0 + gv * (1.0 - sg))).astype(BF))
        d_up.append((d_hidden * active[:, s]).astype(BF))
    d_gate = jnp.concatenate(d_gate, 1)
    d_up = jnp.concatenate(d_up, 1)

    hidden1_all = jnp.concatenate(hidden1, 0)
    hidden2 = over_core(hidden0)
    hidden3 = over_core(hidden1_all)
    mine = [jnp.where(own_near, a, b) for a, b in ((near0, far0), (near1, far1))]
    theirs = [over_core(jnp.where(own_near, b, a)) for a, b in ((near0, far0), (near1, far1))]
    d_weight = weight_grad(keep_own, [hidden0, hidden1_all, hidden2, hidden3], mine + theirs)
    return (output, d_gate, d_up, d_weight)


def solution(mesh):
    fits = mesh.shape["dp"] == 4 and mesh.shape["tensor"] == 4
    return jax.shard_map(
        four_by_four if fits else any_mesh,
        mesh=mesh,
        in_specs=(
            P(("groups", "dp"), "tensor"),
            P(("groups", "dp"), "tensor"),
            P("tensor", "dp"),
            P("tensor", None),
            P(("groups", "dp"), "tensor"),
        ),
        out_specs=(
            P(("groups", "dp"), "tensor"),
            P(("groups", "dp"), "tensor"),
            P(("groups", "dp"), "tensor"),
            P(("groups", "tensor"), "dp"),
        ),
        check_vma=False,
    )
```

time: 474 us -> 283 us (0.60)
  waiting for transfers between devices: 325 us -> 102 us
  starting transfers between devices: 0.16 us -> 73.9 us
  local copies, waits for them, and re-layouts: 42.3 us -> 4.76 us
  Pallas kernels: 0 us -> 31.4 us
  blocking collectives: 29.3 us -> 0 us
  other arithmetic: 6.87 us -> 31.8 us
  matrix products: 56.3 us -> 35.9 us
  between operations: 13.8 us -> 1.3 us
    all_gather x3 -> x0, waiting for transfers between devices: 286 us -> none  [the longest x1 202 us: per_device(): gathered = lax.all_gather(masked, 'dp', axis=1, tiled=True)]
    ppermute x0 -> x37, waiting for transfers between devices: none -> 102 us  [the longest x23 47.1 us: hop(): return lax.ppermute(a, ('dp', 'tensor'), perm)]
    ppermute x0 -> x37, starting transfers between devices: none -> 73.9 us  [the longest x23 40.4 us: hop(): return lax.ppermute(a, ('dp', 'tensor'), perm)]
    reduce_scatter x1 -> x0, waiting for transfers between devices: 37.5 us -> none  [per_device(): lax.psum_scatter(jnp.dot(hidden, gathered, preferred_element_type=jnp.flo...]
    pallas_call x0 -> x2, Pallas kernels: none -> 31.4 us  [the longest x1 16 us: masked_pair(): pl.pallas_call(mask_body, out_shape=jax.ShapeDtypeStruct((rows, 2 * half)...]
    all_to_all x1 -> x0, blocking collectives: 29.3 us -> none  [per_device(): lax.all_to_all(full_grad, 'dp', split_axis=1, concat_axis=0, tiled=True)]
    broadcast_in_dim x4 -> x0, local copies, waits for them, and re-layouts: 22.7 us -> none  [expand_mask(): widened = jnp.repeat(jnp.repeat(small_mask, BLK, axis=0), BLK, axis=1)]
    dot_general x3 -> x11, matrix products: 56.3 us -> 35.9 us  [the longest x4 15.6 us: four_by_four(): lax.dot_general(both0, w, COLS_CONTRACT, preferred_element_type=F32)]
  transfers between devices with their start and end apart: 4 -> 37, of which waited for: 4 -> 11; matrix products, arithmetic and copies ran while one was open for 7% -> 19% of each run, Pallas kernels for 0% -> 6%
where the time goes in v1:
time: 283 us; the launch traced here: 281 us
  waiting for transfers between devices  102 us (36%)
  starting transfers between devices  73.9 us (26%)
  matrix products  35.9 us (13%)
  other arithmetic  31.8 us (11%)
  Pallas kernels  31.4 us (11%)
  local copies, waits for them, and re-layouts  4.76 us (2%)
    ppermute x23, waiting for transfers between devices, hop(): return lax.ppermute(a, ('dp', 'tensor'), perm)  47.1 us
    ppermute x23, starting transfers between devices, hop(): return lax.ppermute(a, ('dp', 'tensor'), perm)  40.4 us
    ppermute x1, waiting for transfers between devices, to_roots(): return lax.ppermute(a, ('dp', 'tensor'), perm)  31.2 us
    ppermute x6, waiting for transfers between devices, over_x(): return lax.ppermute(a, 'dp', [(i, i ^ 2) for i in range(n_dp)])  22.2 us
    ppermute x2, starting transfers between devices, from_roots(): return lax.ppermute(a, ('dp', 'tensor'), perm)  17.3 us
    pallas_call x1, Pallas kernels, masked_pair(): pl.pallas_call(mask_body, out_shape=jax.ShapeDtypeStruct((rows, 2 * half)...  16 us
    dot_general x4, matrix products, four_by_four(): lax.dot_general(both0, w, COLS_CONTRACT, preferred_element_type=F32)  15.6 us
    pallas_call x1, Pallas kernels, weight_grad(): pl.pallas_call(functools.partial(dw_body, n), out_shape=jax.ShapeDtypeStr...  15.5 us
  transfers between devices with their start and end apart: 37, of which 11 were waited for; matrix products, arithmetic and copies ran while one was open for 19% of the time, Pallas kernels for 6%

profile of v1, /device:TPU:0, one launch (start us, length us, event | category | flops | bytes accessed | tf_op | source)
XLA Modules:
  0.0 281.2 jit_solution(4420793642866092275)
XLA Ops:
  1.1 7.1 %convert_multiply_fusion = (f32[256,4096]{1,0:T(8,128)}, bf16[256,4096]{1,0:T(8,128)(2,1)S(1)}, f32[256,4096]{1,0:T(8,128)}) fusion(bf16[256,4096]{1,0:T(8,128)(2,1)} %param.5, bf16[256,4096]{1,0:T(8,128)(2,1)} %param.6), kind=kLoop, calls=%fused_computation.20 | loop fusion | flops 8388608 | bytes 14680064 | tf_op jit(solution)/shard_map/mul | solution.py:186
  8.4 2.6 collective-permute-start.6
  11.1 4.0 %collective-permute-start.21 = (bf16[256,1024]{1,0:T(8,128)(2,1)S(1)}, bf16[256,1024]{1,0:T(8,128)(2,1)S(1)}, u32[]{:S(2)}, u32[]{:S(2)}) collective-permute-start(bf16[256,1024]{1,0:T(8,128)(2,1)S(1)} %copy-done.18), channel_id=1, source_target_pairs={{0,1},{1,2},{4,5},{5,6},{11,10},{10,9},{15,14},{14,13},{16,17},{17... | collective-permute-start | bytes 1572872 | tf_op jit(solution)/shard_map/ppermute | solution.py:152
  16.4 18.7 %collective-permute-done.6 = bf16[128,4096]{1,0:T(8,128)(2,1)S(1)} collective-permute-done((bf16[128,4096]{1,0:T(8,128)(2,1)S(1)}, bf16[128,4096]{1,0:T(8,128)(2,1)S(1)}, u32[]{:S(2)}, u32[]{:S(2)}) %collective-permute-start.6) | collective-permute-done | bytes 1048608 | tf_op jit(solution)/shard_map/ppermute | solution.py:155
  37.4 31.2 %collective-permute-done.24 = bf16[256,1024]{1,0:T(8,128)(2,1)S(1)} collective-permute-done((bf16[256,1024]{1,0:T(8,128)(2,1)S(1)}, bf16[256,1024]{1,0:T(8,128)(2,1)S(1)}, u32[]{:S(2)}, u32[]{:S(2)}) %collective-permute-start.24) | collective-permute-done | bytes 524320 | tf_op jit(solution)/shard_map/ppermute | solution.py:164
  70.0 6.4 %collective-permute-start.26 = (bf16[256,1024]{1,0:T(8,128)(2,1)S(1)}, bf16[256,1024]{1,0:T(8,128)(2,1)}, u32[]{:S(2)}, u32[]{:S(2)}) collective-permute-start(bf16[256,1024]{1,0:T(8,128)(2,1)S(1)} %collective-permute-done.24), channel_id=1, source_target_pairs={{0,1},{1,2},{4,5},{5,6},{11,10},{10,9},{15,14},{14,13},{16,17},{17... | collective-permute-start | bytes 1572872 | tf_op jit(solution)/shard_map/ppermute | solution.py:152
  79.0 7.3 %collective-permute-done.26 = bf16[256,1024]{1,0:T(8,128)(2,1)} collective-permute-done((bf16[256,1024]{1,0:T(8,128)(2,1)S(1)}, bf16[256,1024]{1,0:T(8,128)(2,1)}, u32[]{:S(2)}, u32[]{:S(2)}) %collective-permute-start.26) | collective-permute-done | bytes 524320 | tf_op jit(solution)/shard_map/ppermute | solution.py:152
  87.8 4.3 %convert_element_type.159 = f32[256,4096]{1,0:T(8,128)} convert(bf16[256,4096]{1,0:T(8,128)(2,1)} %param.5) | non-fusion elementwise | flops 1048576 | bytes 6291456 | tf_op jit(solution)/shard_map/convert_element_type | solution.py:183
  92.1 2.5 convert_element_type.160
  98.7 20.7 %collective-permute-done.25 = bf16[256,1024]{1,0:T(8,128)(2,1)S(1)} collective-permute-done((bf16[256,1024]{1,0:T(8,128)(2,1)}, bf16[256,1024]{1,0:T(8,128)(2,1)S(1)}, u32[]{:S(2)}, u32[]{:S(2)}) %collective-permute-start.25) | collective-permute-done | bytes 524320 | tf_op jit(solution)/shard_map/ppermute | solution.py:152
  123.0 15.5 %weight_grad.1 = f32[4096,1024]{1,0:T(8,128)} custom-call(s32[32,8]{1,0:T(8,128)S(1)} %get-tuple-element.35.keep_ref, bf16[256,4096]{1,0:T(8,128)(2,1)S(1)} %get-tuple-element.19.refs_0_, bf16[256,4096]{1,0:T(8,128)(2,1)} %constant_dynamic-update-slice_fusion.refs_1_, bf16[256,4096]{1,0:T(8,128)(2,1)} %collective-permute-done.33.refs_2_, ...), custom_call_target="tpu_custom_call" | custom-call | tf_op jit(solution)/shard_map/weight_grad/pallas_call | solution.py:120
  138.6 16.0 %masked_pair.1 = bf16[4096,2048]{1,0:T(8,128)(2,1)} custom-call(s32[33,16]{1,0:T(8,128)S(1)} %concatenate.25.info, bf16[4096,1024]{1,0:T(8,128)(2,1)S(1)} %bitcast.7, bf16[4096,1024]{1,0:T(8,128)(2,1)} %collective-permute-done.other), custom_call_target="tpu_custom_call" | custom-call | tf_op jit(solution)/shard_map/masked_pair/pallas_call | solution.py:84
  154.5 3.6 %fusion.28 = bf16[256,1024]{1,0:T(8,128)(2,1)S(1)} fusion(bf16[4096,2048]{1,0:T(8,128)(2,1)} %masked_pair.1, bf16[256,1024]{1,0:T(8,128)(2,1)S(1)} %copy-done.11, bf16[256,1024]{1,0:T(8,128)(2,1)S(1)} %copy-done.9), kind=kOutput, calls=%fused_computation.25 | convolution fusion | flops 1076101120 | bytes 5767168 | tf_op jit(solution)/shard_map/dot_general | solution.py:222
  158.2 4.2 %fusion.31 = bf16[256,1024]{1,0:T(8,128)(2,1)S(1)} fusion(bf16[4096,2048]{1,0:T(8,128)(2,1)} %masked_pair.1, bf16[256,1024]{1,0:T(8,128)(2,1)S(1)} %copy-done.11, bf16[256,1024]{1,0:T(8,128)(2,1)S(1)} %copy-done.9), kind=kOutput, calls=%fused_computation.26 | convolution fusion | flops 1076101120 | bytes 5767168 | tf_op jit(solution)/shard_map/dot_general | solution.py:222
  165.7 4.7 %fusion.68 = f32[256,2048]{1,0:T(8,128)S(1)} fusion(bf16[256,4096]{1,0:T(8,128)(2,1)S(1)} %get-tuple-element.19.refs_0_, bf16[4096,2048]{1,0:T(8,128)(2,1)S(1)} %copy-done), kind=kOutput, calls=%fused_computation.103 | convolution fusion | flops 4294967296 | bytes 20971520 | tf_op jit(solution)/shard_map/dot_general | solution.py:200
  170.3 6.2 %collective-permute-start.32 = (bf16[256,1024]{1,0:T(8,128)(2,1)S(1)}, bf16[256,1024]{1,0:T(8,128)(2,1)S(1)}, u32[]{:S(2)}, u32[]{:S(2)}) collective-permute-start(bf16[256,1024]{1,0:T(8,128)(2,1)S(1)} %fusion.37), channel_id=1, source_target_pairs={{0,8},{4,12},{8,0},{12,4},{1,9},{5,13},{9,1},{13,5},{2,10},{6,14},... | collective-permute-start | bytes 1572872 | tf_op jit(solution)/shard_map/ppermute | solution.py:155
  178.5 2.5 fusion.69
  182.0 2.5 fusion.70
  186.4 2.9 %collective-permute-start.29 = (bf16[256,1024]{1,0:T(8,128)(2,1)S(1)}, bf16[256,1024]{1,0:T(8,128)(2,1)S(1)}, u32[]{:S(2)}, u32[]{:S(2)}) collective-permute-start(bf16[256,1024]{1,0:T(8,128)(2,1)S(1)} %fusion.28), channel_id=1, source_target_pairs={{0,8},{4,12},{8,0},{12,4},{1,9},{5,13},{9,1},{13,5},{2,10},{6,14},... | collective-permute-start | bytes 1572872 | tf_op jit(solution)/shard_map/ppermute | solution.py:155
  190.2 4.4 %collective-permute-start.4 = (bf16[256,1024]{1,0:T(8,128)(2,1)}, bf16[256,1024]{1,0:T(8,128)(2,1)S(1)}, u32[]{:S(2)}, u32[]{:S(2)}) collective-permute-start(bf16[256,1024]{1,0:T(8,128)(2,1)} %get-tuple-element.26), channel_id=1, source_target_pairs={{3,2},{0,1},{7,6},{4,5},{8,9},{11,10},{12,13},{15,14},{19,18},{16,... | collective-permute-start | bytes 1572872 | tf_op jit(solution)/shard_map/ppermute | solution.py:152
  194.6 2.3 fusion.25
  196.9 3.5 %collective-permute-done.31 = bf16[256,1024]{1,0:T(8,128)(2,1)S(1)} collective-permute-done((bf16[256,1024]{1,0:T(8,128)(2,1)S(1)}, bf16[256,1024]{1,0:T(8,128)(2,1)S(1)}, u32[]{:S(2)}, u32[]{:S(2)}) %collective-permute-start.31) | collective-permute-done | bytes 524320 | tf_op jit(solution)/shard_map/ppermute | solution.py:155
  202.0 2.3 fusion.22
  206.0 2.8 %collective-permute-done.10 = bf16[128,1024]{1,0:T(8,128)(2,1)S(1)} collective-permute-done((bf16[128,1024]{1,0:T(8,128)(2,1)S(1)}, bf16[128,1024]{1,0:T(8,128)(2,1)S(1)}, u32[]{:S(2)}, u32[]{:S(2)}) %collective-permute-start.10) | collective-permute-done | bytes 262176 | tf_op jit(solution)/shard_map/ppermute | solution.py:152
  208.8 4.4 %collective-permute-start.17 = (bf16[128,1024]{1,0:T(8,128)(2,1)S(1)}, bf16[128,1024]{1,0:T(8,128)(2,1)S(1)}, u32[]{:S(2)}, u32[]{:S(2)}) collective-permute-start(bf16[128,1024]{1,0:T(8,128)(2,1)S(1)} %get-tuple-element.34), channel_id=1, source_target_pairs={{3,2},{0,1},{7,6},{4,5},{8,9},{11,10},{12,13},{15,14},{19,18},{16,... | collective-permute-start | bytes 786440 | tf_op jit(solution)/shard_map/ppermute | solution.py:152
  214.9 2.2 collective-permute-done.17
  222.2 2.3 fusion.19
  226.7 8.6 %fusion.58 = (bf16[256,1024]{1,0:T(8,128)(2,1)}, bf16[256,1024]{1,0:T(8,128)(2,1)}, bf16[256,1024]{1,0:T(8,128)(2,1)}, bf16[256,1024]{1,0:T(8,128)(2,1)}, f32[256,1024]{1,0:T(8,128)}) fusion(f32[256,4096]{1,0:T(8,128)} %convert_element_type.159, f32[256,4096]{1,0:T(8,128)} %convert_element_type.160, f32[256,4096]{1,0:T(8,128)} %get-tuple-element.20, ...), kind=kOutput, calls=%fused_computation.58 | convolution fusion | flops 1083703296 | bytes 24641536 | tf_op jit(solution)/shard_map/dot_general | solution.py:224
  235.2 4.2 %fusion.43 = (bf16[256,1024]{1,0:T(8,128)(2,1)S(1)}, bf16[256,1024]{1,0:T(8,128)(2,1)S(1)}, bf16[256,1024]{1,0:T(8,128)(2,1)S(1)}, bf16[256,1024]{1,0:T(8,128)(2,1)S(1)}) fusion(f32[256,1024]{1,0:T(8,128)} %get-tuple-element.38, f32[256,4096]{1,0:T(8,128)} %get-tuple-element.18, f32[256,1024]{1,0:T(8,128)} %fusion.22, f32[256,1024]{1,0:T(8,128)} %fusion.19, ...), kind=kLoop, calls=%fused_computation.36 | loop fusion | flops 2097152 | bytes 10485760 | tf_op jit(solution)/shard_map/convert_element_type | solution.py:228
  239.4 2.4 collective-permute-done.9
  243.8 16.0 %collective-permute-start.12 = (bf16[128,1024]{1,0:T(8,128)(2,1)S(1)}, bf16[128,1024]{1,0:T(8,128)(2,1)S(1)}, u32[]{:S(2)}, u32[]{:S(2)}) collective-permute-start(bf16[128,1024]{1,0:T(8,128)(2,1)S(1)} %select_convert_fusion.2), channel_id=1, source_target_pairs={{0,8},{1,9},{4,12},{5,13},{11,3},{10,2},{15,7},{14,6},{16,24},{17,... | collective-permute-start | bytes 786440 | tf_op jit(solution)/shard_map/ppermute | solution.py:168
  268.3 11.6 %collective-permute-done.3 = bf16[256,1024]{1,0:T(8,128)(2,1)S(1)} collective-permute-done((bf16[256,1024]{1,0:T(8,128)(2,1)S(1)}, bf16[256,1024]{1,0:T(8,128)(2,1)S(1)}, u32[]{:S(2)}, u32[]{:S(2)}) %collective-permute-start.3) | collective-permute-done | bytes 524320 | tf_op jit(solution)/shard_map/ppermute | solution.py:152
  (139 shorter events, 50.1 us)
Async XLA Ops:
  0.6 137.9 %collective-permute-start = (bf16[4096,1024]{1,0:T(8,128)(2,1)}, bf16[4096,1024]{1,0:T(8,128)(2,1)}, u32[]{:S(2)}, u32[]{:S(2)}) collective-permute-start(bf16[4096,1024]{1,0:T(8,128)(2,1)} %own.1), channel_id=1, source_target_pairs={{0,4},{4,0},{8,12},{12,8},{1,5},{5,1},{9,13},{13,9},{2,6},{6,2},{1... | collective-permute-start | bytes 25165832 | tf_op jit(solution)/shard_map/ppermute | solution.py:158
  8.4 26.6 %collective-permute-start.6 = (bf16[128,4096]{1,0:T(8,128)(2,1)S(1)}, bf16[128,4096]{1,0:T(8,128)(2,1)S(1)}, u32[]{:S(2)}, u32[]{:S(2)}) collective-permute-start(bf16[128,4096]{1,0:T(8,128)(2,1)S(1)} %get-tuple-element.21), channel_id=1, source_target_pairs={{0,8},{4,12},{8,0},{12,4},{1,9},{5,13},{9,1},{13,5},{2,10},{6,14},... | collective-permute-start | bytes 3145736 | tf_op jit(solution)/shard_map/ppermute | solution.py:155
  11.0 59.0 %collective-permute-start.13 = (bf16[128,4096]{1,0:T(8,128)(2,1)S(1)}, bf16[128,4096]{1,0:T(8,128)(2,1)S(1)}, u32[]{:S(2)}, u32[]{:S(2)}) collective-permute-start(bf16[128,4096]{1,0:T(8,128)(2,1)S(1)} %get-tuple-element.22), channel_id=1, source_target_pairs={{0,8},{4,12},{8,0},{12,4},{1,9},{5,13},{9,1},{13,5},{2,10},{6,14},... | collective-permute-start | bytes 3145736 | tf_op jit(solution)/shard_map/ppermute | solution.py:155
  11.1 26.3 %collective-permute-start.21 = (bf16[256,1024]{1,0:T(8,128)(2,1)S(1)}, bf16[256,1024]{1,0:T(8,128)(2,1)S(1)}, u32[]{:S(2)}, u32[]{:S(2)}) collective-permute-start(bf16[256,1024]{1,0:T(8,128)(2,1)S(1)} %copy-done.18), channel_id=1, source_target_pairs={{0,1},{1,2},{4,5},{5,6},{11,10},{10,9},{15,14},{14,13},{16,17},{17... | collective-permute-start | bytes 1572872 | tf_op jit(solution)/shard_map/ppermute | solution.py:152
  15.1 53.5 %collective-permute-start.24 = (bf16[256,1024]{1,0:T(8,128)(2,1)S(1)}, bf16[256,1024]{1,0:T(8,128)(2,1)S(1)}, u32[]{:S(2)}, u32[]{:S(2)}) collective-permute-start(bf16[256,1024]{1,0:T(8,128)(2,1)S(1)} %copy-done.18), channel_id=1, source_target_pairs={{8,0},{9,1},{12,4},{13,5},{3,11},{2,10},{7,15},{6,14},{24,16},{25,... | collective-permute-start | bytes 1572872 | tf_op jit(solution)/shard_map/ppermute | solution.py:164
  35.0 42.4 %collective-permute-start.20 = (bf16[256,1024]{1,0:T(8,128)(2,1)S(1)}, bf16[256,1024]{1,0:T(8,128)(2,1)S(1)}, u32[]{:S(2)}, u32[]{:S(2)}) collective-permute-start(bf16[256,1024]{1,0:T(8,128)(2,1)S(1)} %copy-done.18), channel_id=1, source_target_pairs={{1,0},{5,4},{10,11},{14,15},{17,16},{21,20},{26,27},{30,31}} | collective-permute-start | bytes 1572872 | tf_op jit(solution)/shard_map/ppermute | solution.py:152
  37.4 84.3 %collective-permute-start.33 = (bf16[256,4096]{1,0:T(8,128)(2,1)S(1)}, bf16[256,4096]{1,0:T(8,128)(2,1)}, u32[]{:S(2)}, u32[]{:S(2)}) collective-permute-start(bf16[256,4096]{1,0:T(8,128)(2,1)S(1)} %get-tuple-element.19.refs_0_), channel_id=1, source_target_pairs={{0,4},{4,0},{8,12},{12,8},{1,5},{5,1},{9,13},{13,9},{2,6},{6,2},{1... | collective-permute-start | bytes 6291464 | tf_op jit(solution)/shard_map/ppermute | solution.py:158
  68.5 9.0 %collective-permute-start.22 = (bf16[256,1024]{1,0:T(8,128)(2,1)S(1)}, bf16[256,1024]{1,0:T(8,128)(2,1)}, u32[]{:S(2)}, u32[]{:S(2)}) collective-permute-start(bf16[256,1024]{1,0:T(8,128)(2,1)S(1)} %collective-permute-done.21), channel_id=1, source_target_pairs={{1,2},{2,3},{5,6},{6,7},{10,9},{9,8},{14,13},{13,12},{17,18},{18,1... | collective-permute-start | bytes 1572872 | tf_op jit(solution)/shard_map/ppermute | solution.py:152
  70.0 16.3 %collective-permute-start.26 = (bf16[256,1024]{1,0:T(8,128)(2,1)S(1)}, bf16[256,1024]{1,0:T(8,128)(2,1)}, u32[]{:S(2)}, u32[]{:S(2)}) collective-permute-start(bf16[256,1024]{1,0:T(8,128)(2,1)S(1)} %collective-permute-done.24), channel_id=1, source_target_pairs={{0,1},{1,2},{4,5},{5,6},{11,10},{10,9},{15,14},{14,13},{16,17},{17... | collective-permute-start | bytes 1572872 | tf_op jit(solution)/shard_map/ppermute | solution.py:152
  77.4 45.6 %collective-permute-start.34 = (bf16[256,4096]{1,0:T(8,128)(2,1)}, bf16[256,4096]{1,0:T(8,128)(2,1)}, u32[]{:S(2)}, u32[]{:S(2)}) collective-permute-start(bf16[256,4096]{1,0:T(8,128)(2,1)} %constant_dynamic-update-slice_fusion.refs_1_), channel_id=1, source_target_pairs={{0,4},{4,0},{8,12},{12,8},{1,5},{5,1},{9,13},{13,9},{2,6},{6,2},{1... | collective-permute-start | bytes 6291464 | tf_op jit(solution)/shard_map/ppermute | solution.py:158
  77.5 17.1 %collective-permute-start.23 = (bf16[256,1024]{1,0:T(8,128)(2,1)}, bf16[256,1024]{1,0:T(8,128)(2,1)}, u32[]{:S(2)}, u32[]{:S(2)}) collective-permute-start(bf16[256,1024]{1,0:T(8,128)(2,1)} %collective-permute-done.22), channel_id=1, source_target_pairs={{2,3},{6,7},{9,8},{13,12},{18,19},{22,23},{25,24},{29,28}} | collective-permute-start | bytes 1572872 | tf_op jit(solution)/shard_map/ppermute | solution.py:152
  86.3 9.7 %collective-permute-start.27 = (bf16[256,1024]{1,0:T(8,128)(2,1)}, bf16[256,1024]{1,0:T(8,128)(2,1)}, u32[]{:S(2)}, u32[]{:S(2)}) collective-permute-start(bf16[256,1024]{1,0:T(8,128)(2,1)} %collective-permute-done.26), channel_id=1, source_target_pairs={{1,2},{2,3},{5,6},{6,7},{10,9},{9,8},{14,13},{13,12},{17,18},{18,1... | collective-permute-start | bytes 1572872 | tf_op jit(solution)/shard_map/ppermute | solution.py:152
  94.6 24.9 %collective-permute-start.25 = (bf16[256,1024]{1,0:T(8,128)(2,1)}, bf16[256,1024]{1,0:T(8,128)(2,1)S(1)}, u32[]{:S(2)}, u32[]{:S(2)}) collective-permute-start(bf16[256,1024]{1,0:T(8,128)(2,1)} %copy-done.19), channel_id=1, source_target_pairs={{1,0},{5,4},{10,11},{14,15},{17,16},{21,20},{26,27},{30,31}} | collective-permute-start | bytes 1572872 | tf_op jit(solution)/shard_map/ppermute | solution.py:152
  96.0 23.5 %collective-permute-start.28 = (bf16[256,1024]{1,0:T(8,128)(2,1)}, bf16[256,1024]{1,0:T(8,128)(2,1)S(1)}, u32[]{:S(2)}, u32[]{:S(2)}) collective-permute-start(bf16[256,1024]{1,0:T(8,128)(2,1)} %collective-permute-done.27), channel_id=1, source_target_pairs={{2,3},{6,7},{9,8},{13,12},{18,19},{22,23},{25,24},{29,28}} | collective-permute-start | bytes 1572872 | tf_op jit(solution)/shard_map/ppermute | solution.py:152
  170.3 19.8 %collective-permute-start.32 = (bf16[256,1024]{1,0:T(8,128)(2,1)S(1)}, bf16[256,1024]{1,0:T(8,128)(2,1)S(1)}, u32[]{:S(2)}, u32[]{:S(2)}) collective-permute-start(bf16[256,1024]{1,0:T(8,128)(2,1)S(1)} %fusion.37), channel_id=1, source_target_pairs={{0,8},{4,12},{8,0},{12,4},{1,9},{5,13},{9,1},{13,5},{2,10},{6,14},... | collective-permute-start | bytes 1572872 | tf_op jit(solution)/shard_map/ppermute | solution.py:155
  176.5 24.0 %collective-permute-start.31 = (bf16[256,1024]{1,0:T(8,128)(2,1)S(1)}, bf16[256,1024]{1,0:T(8,128)(2,1)S(1)}, u32[]{:S(2)}, u32[]{:S(2)}) collective-permute-start(bf16[256,1024]{1,0:T(8,128)(2,1)S(1)} %fusion.34), channel_id=1, source_target_pairs={{0,8},{4,12},{8,0},{12,4},{1,9},{5,13},{9,1},{13,5},{2,10},{6,14},... | collective-permute-start | bytes 1572872 | tf_op jit(solution)/shard_map/ppermute | solution.py:155
  176.6 44.3 %collective-permute-start.30 = (bf16[256,1024]{1,0:T(8,128)(2,1)S(1)}, bf16[256,1024]{1,0:T(8,128)(2,1)S(1)}, u32[]{:S(2)}, u32[]{:S(2)}) collective-permute-start(bf16[256,1024]{1,0:T(8,128)(2,1)S(1)} %fusion.31), channel_id=1, source_target_pairs={{0,8},{4,12},{8,0},{12,4},{1,9},{5,13},{9,1},{13,5},{2,10},{6,14},... | collective-permute-start | bytes 1572872 | tf_op jit(solution)/shard_map/ppermute | solution.py:155
  186.4 38.1 %collective-permute-start.29 = (bf16[256,1024]{1,0:T(8,128)(2,1)S(1)}, bf16[256,1024]{1,0:T(8,128)(2,1)S(1)}, u32[]{:S(2)}, u32[]{:S(2)}) collective-permute-start(bf16[256,1024]{1,0:T(8,128)(2,1)S(1)} %fusion.28), channel_id=1, source_target_pairs={{0,8},{4,12},{8,0},{12,4},{1,9},{5,13},{9,1},{13,5},{2,10},{6,14},... | collective-permute-start | bytes 1572872 | tf_op jit(solution)/shard_map/ppermute | solution.py:155
  189.4 15.0 %collective-permute-start.1 = (bf16[256,1024]{1,0:T(8,128)(2,1)S(1)}, bf16[256,1024]{1,0:T(8,128)(2,1)S(1)}, u32[]{:S(2)}, u32[]{:S(2)}) collective-permute-start(bf16[256,1024]{1,0:T(8,128)(2,1)S(1)} %get-tuple-element.25), channel_id=1, source_target_pairs={{3,2},{7,6},{8,9},{12,13},{19,18},{23,22},{24,25},{28,29}} | collective-permute-start | bytes 1572872 | tf_op jit(solution)/shard_map/ppermute | solution.py:152
  190.2 72.2 %collective-permute-start.4 = (bf16[256,1024]{1,0:T(8,128)(2,1)}, bf16[256,1024]{1,0:T(8,128)(2,1)S(1)}, u32[]{:S(2)}, u32[]{:S(2)}) collective-permute-start(bf16[256,1024]{1,0:T(8,128)(2,1)} %get-tuple-element.26), channel_id=1, source_target_pairs={{3,2},{0,1},{7,6},{4,5},{8,9},{11,10},{12,13},{15,14},{19,18},{16,... | collective-permute-start | bytes 1572872 | tf_op jit(solution)/shard_map/ppermute | solution.py:152
  200.5 8.4 %collective-permute-start.10 = (bf16[128,1024]{1,0:T(8,128)(2,1)S(1)}, bf16[128,1024]{1,0:T(8,128)(2,1)S(1)}, u32[]{:S(2)}, u32[]{:S(2)}) collective-permute-start(bf16[128,1024]{1,0:T(8,128)(2,1)S(1)} %get-tuple-element.30), channel_id=1, source_target_pairs={{3,2},{0,1},{7,6},{4,5},{8,9},{11,10},{12,13},{15,14},{19,18},{16,... | collective-permute-start | bytes 786440 | tf_op jit(solution)/shard_map/ppermute | solution.py:152
  204.4 8.9 %collective-permute-start.8 = (bf16[128,1024]{1,0:T(8,128)(2,1)S(1)}, bf16[128,1024]{1,0:T(8,128)(2,1)S(1)}, u32[]{:S(2)}, u32[]{:S(2)}) collective-permute-start(bf16[128,1024]{1,0:T(8,128)(2,1)S(1)} %add_convert_fusion.5), channel_id=1, source_target_pairs={{2,1},{6,5},{9,10},{13,14},{18,17},{22,21},{25,26},{29,30}} | collective-permute-start | bytes 786440 | tf_op jit(solution)/shard_map/ppermute | solution.py:152
  208.8 8.3 %collective-permute-start.17 = (bf16[128,1024]{1,0:T(8,128)(2,1)S(1)}, bf16[128,1024]{1,0:T(8,128)(2,1)S(1)}, u32[]{:S(2)}, u32[]{:S(2)}) collective-permute-start(bf16[128,1024]{1,0:T(8,128)(2,1)S(1)} %get-tuple-element.34), channel_id=1, source_target_pairs={{3,2},{0,1},{7,6},{4,5},{8,9},{11,10},{12,13},{15,14},{19,18},{16,... | collective-permute-start | bytes 786440 | tf_op jit(solution)/shard_map/ppermute | solution.py:152
  217.1 45.3 %collective-permute-start.2 = (bf16[256,1024]{1,0:T(8,128)(2,1)}, bf16[256,1024]{1,0:T(8,128)(2,1)}, u32[]{:S(2)}, u32[]{:S(2)}) collective-permute-start(bf16[256,1024]{1,0:T(8,128)(2,1)} %add_convert_fusion.1), channel_id=1, source_target_pairs={{2,1},{6,5},{9,10},{13,14},{18,17},{22,21},{25,26},{29,30}} | collective-permute-start | bytes 1572872 | tf_op jit(solution)/shard_map/ppermute | solution.py:152
  218.6 23.2 %collective-permute-start.9 = (bf16[128,1024]{1,0:T(8,128)(2,1)}, bf16[128,1024]{1,0:T(8,128)(2,1)}, u32[]{:S(2)}, u32[]{:S(2)}) collective-permute-start(bf16[128,1024]{1,0:T(8,128)(2,1)} %get-tuple-element.27), channel_id=1, source_target_pairs={{1,0},{5,4},{10,11},{14,15},{17,16},{21,20},{26,27},{30,31}} | collective-permute-start | bytes 786440 | tf_op jit(solution)/shard_map/ppermute | solution.py:152
  220.9 21.8 %collective-permute-start.11 = (bf16[128,1024]{1,0:T(8,128)(2,1)}, bf16[128,1024]{1,0:T(8,128)(2,1)}, u32[]{:S(2)}, u32[]{:S(2)}) collective-permute-start(bf16[128,1024]{1,0:T(8,128)(2,1)} %get-tuple-element.28), channel_id=1, source_target_pairs={{2,1},{6,5},{9,10},{13,14},{18,17},{22,21},{25,26},{29,30}} | collective-permute-start | bytes 786440 | tf_op jit(solution)/shard_map/ppermute | solution.py:152
  225.4 34.5 %collective-permute-start.16 = (bf16[128,1024]{1,0:T(8,128)(2,1)}, bf16[128,1024]{1,0:T(8,128)(2,1)}, u32[]{:S(2)}, u32[]{:S(2)}) collective-permute-start(bf16[128,1024]{1,0:T(8,128)(2,1)} %get-tuple-element.31), channel_id=1, source_target_pairs={{1,0},{5,4},{10,11},{14,15},{17,16},{21,20},{26,27},{30,31}} | collective-permute-start | bytes 786440 | tf_op jit(solution)/shard_map/ppermute | solution.py:152
  241.8 18.1 %collective-permute-start.18 = (bf16[128,1024]{1,0:T(8,128)(2,1)S(1)}, bf16[128,1024]{1,0:T(8,128)(2,1)S(1)}, u32[]{:S(2)}, u32[]{:S(2)}) collective-permute-start(bf16[128,1024]{1,0:T(8,128)(2,1)S(1)} %copy-done.23), channel_id=1, source_target_pairs={{2,1},{6,5},{9,10},{13,14},{18,17},{22,21},{25,26},{29,30}} | collective-permute-start | bytes 786440 | tf_op jit(solution)/shard_map/ppermute | solution.py:152
  243.8 24.2 %collective-permute-start.12 = (bf16[128,1024]{1,0:T(8,128)(2,1)S(1)}, bf16[128,1024]{1,0:T(8,128)(2,1)S(1)}, u32[]{:S(2)}, u32[]{:S(2)}) collective-permute-start(bf16[128,1024]{1,0:T(8,128)(2,1)S(1)} %select_convert_fusion.2), channel_id=1, source_target_pairs={{0,8},{1,9},{4,12},{5,13},{11,3},{10,2},{15,7},{14,6},{16,24},{17,... | collective-permute-start | bytes 786440 | tf_op jit(solution)/shard_map/ppermute | solution.py:168
  261.0 7.2 %collective-permute-start.19 = (bf16[128,1024]{1,0:T(8,128)(2,1)S(1)}, bf16[128,1024]{1,0:T(8,128)(2,1)S(1)}, u32[]{:S(2)}, u32[]{:S(2)}) collective-permute-start(bf16[128,1024]{1,0:T(8,128)(2,1)S(1)} %select_convert_fusion.1), channel_id=1, source_target_pairs={{0,8},{1,9},{4,12},{5,13},{11,3},{10,2},{15,7},{14,6},{16,24},{17,... | collective-permute-start | bytes 786440 | tf_op jit(solution)/shard_map/ppermute | solution.py:168
  263.8 16.1 %collective-permute-start.3 = (bf16[256,1024]{1,0:T(8,128)(2,1)S(1)}, bf16[256,1024]{1,0:T(8,128)(2,1)S(1)}, u32[]{:S(2)}, u32[]{:S(2)}) collective-permute-start(bf16[256,1024]{1,0:T(8,128)(2,1)S(1)} %get-tuple-element.23), channel_id=1, source_target_pairs={{1,0},{5,4},{10,11},{14,15},{17,16},{21,20},{26,27},{30,31}} | collective-permute-start | bytes 1572872 | tf_op jit(solution)/shard_map/ppermute | solution.py:152
  265.1 14.8 %collective-permute-start.5 = (bf16[256,1024]{1,0:T(8,128)(2,1)S(1)}, bf16[256,1024]{1,0:T(8,128)(2,1)S(1)}, u32[]{:S(2)}, u32[]{:S(2)}) collective-permute-start(bf16[256,1024]{1,0:T(8,128)(2,1)S(1)} %get-tuple-element.24), channel_id=1, source_target_pairs={{2,1},{6,5},{9,10},{13,14},{18,17},{22,21},{25,26},{29,30}} | collective-permute-start | bytes 1572872 | tf_op jit(solution)/shard_map/ppermute | solution.py:152
  (33 other events, 476.9 us)

commit v2 on v0

v2 whole, which is shorter than its diff:
```python
import math

import jax
import jax.numpy as jnp
from jax import lax
from jax.experimental import pallas as pl
from jax.experimental.pallas import tpu as pltpu
from jax.sharding import PartitionSpec as P

BLK = 128
BF = jnp.bfloat16
F32 = jnp.float32
ROWS_CONTRACT = (((0,), (0,)), ((), ()))
COLS_CONTRACT = (((1,), (1,)), ((), ()))


def expand_mask(small_mask):
    widened = jnp.repeat(jnp.repeat(small_mask, BLK, axis=0), BLK, axis=1)
    return widened


def any_mesh(gate_pre, up_pre, down_weight, block_mask, grad_out):
    d_local = down_weight.shape[1]
    d_blocks = d_local // BLK
    own_mask = lax.dynamic_slice_in_dim(block_mask, lax.axis_index("dp") * d_blocks, d_blocks, 1)
    keep_wide = expand_mask(own_mask)
    masked = down_weight * keep_wide.astype(BF)
    gate_val = gate_pre.astype(F32)
    up_val = up_pre.astype(F32)
    gate_sig = jax.nn.sigmoid(gate_val)
    active = gate_val * gate_sig
    hidden = (active * up_val).astype(BF)
    full_grad = lax.all_gather(grad_out, "tensor", axis=1, tiled=True)
    gathered = lax.all_gather(masked, "dp", axis=1, tiled=True)
    d_hidden = lax.dot_general(full_grad, gathered, COLS_CONTRACT, preferred_element_type=F32)
    output = lax.psum_scatter(
        jnp.dot(hidden, gathered, preferred_element_type=F32),
        "tensor",
        scatter_dimension=1,
        tiled=True,
    ).astype(BF)
    d_gate = (d_hidden * up_val * gate_sig * (1.0 + gate_val * (1.0 - gate_sig))).astype(BF)
    d_up = (d_hidden * active).astype(BF)
    grad_cols = lax.all_to_all(full_grad, "dp", split_axis=1, concat_axis=0, tiled=True)
    d_weight = lax.dot_general(
        lax.all_gather(hidden, "dp", axis=0, tiled=True),
        grad_cols,
        ROWS_CONTRACT,
        preferred_element_type=F32,
    )
    d_weight = d_weight * keep_wide.astype(F32)
    return (output, d_gate, d_up, d_weight)


IN_VMEM = pl.BlockSpec(memory_space=pltpu.VMEM)
IN_SMEM = pl.BlockSpec(memory_space=pltpu.SMEM)
ANYWHERE = pl.BlockSpec(memory_space=pl.ANY)


LARGE = 1536 * 1024


def shaped(shape, dtype):
    size = math.prod(shape) * jnp.dtype(dtype).itemsize
    return (pltpu.HBM if size >= LARGE else jax.ShapeDtypeStruct)(shape, dtype)


def placed(a):
    return pltpu.with_memory_space_constraint(a, pltpu.HBM) if a.size * a.dtype.itemsize >= LARGE else a


def ordered(body, deps, operands, out_shape, *, name, pair=None, flops=1, in_specs=None, out_specs=None, grid=(), scratch=(), aliases=None):
    n, m = len(operands), len(deps)
    one = not isinstance(out_shape, (list, tuple))
    operands = [a if a is pair else placed(a) for a in operands]
    deps = [placed(a) for a in deps]

    def run(*refs):
        body(*refs[:n], *refs[n + m :])

    in_specs = [IN_VMEM] * n if in_specs is None else list(in_specs)
    if out_specs is None:
        out_specs = IN_VMEM if one else [IN_VMEM] * len(out_shape)
    return pl.pallas_call(
        run,
        grid=grid,
        in_specs=in_specs + [ANYWHERE] * m,
        out_specs=out_specs,
        out_shape=out_shape,
        scratch_shapes=scratch,
        input_output_aliases=aliases or {},
        compiler_params=pltpu.CompilerParams(vmem_limit_bytes=18 * 2**20),
        cost_estimate=pl.CostEstimate(flops=flops, bytes_accessed=1, transcendentals=0),
        name=name,
    )(*operands, *deps)


def kept(w, mask_ref, row, first, rep):
    n, cols = w.shape[0] // BLK, w.shape[1]
    out = []
    for r in range(n):
        keep = [jnp.full((rep, BLK), mask_ref[row + r, first + k].astype(F32)) for k in range(cols // BLK)]
        m = jnp.concatenate(keep, 1).astype(w.dtype).reshape(1, rep, cols)
        rows = w[r * BLK : (r + 1) * BLK, :].reshape(BLK // rep, rep, cols) * m
        out.append(rows.reshape(BLK, cols))
    return jnp.concatenate(out, 0)


def hidden_of(gate, up, deps):
    rows, hid = gate.shape
    unit = 64

    def body(gate_ref, up_ref, out):
        g = gate_ref[...].astype(F32)
        out[...] = (g * jax.nn.sigmoid(g) * up_ref[...].astype(F32)).astype(BF)

    at = pl.BlockSpec((unit, hid), lambda i: (i, 0))
    return ordered(
        body,
        deps,
        [gate, up],
        shaped((rows, hid), BF),
        grid=(rows // unit,),
        in_specs=[at, at],
        out_specs=at,
        name="hidden",
    )


def masked_pair(info, mask, own, other, deps):
    hid, cols = own.shape
    step = 512

    def body(info_ref, mask_ref, a, b, out):
        row = pl.program_id(0) * (step // BLK)
        x, core = info_ref[0], info_ref[1]
        out[core] = kept(a[...], mask_ref, row, (2 * x + core) * (cols // BLK), 16)
        out[1 - core] = kept(b[...], mask_ref, row, (2 * x + 1 - core) * (cols // BLK), 16)

    w = pl.BlockSpec((step, cols), lambda k: (k, 0))
    pair = ordered(
        body,
        deps,
        [info, mask, own, other],
        pltpu.VMEM((2, hid, cols), BF),
        grid=(hid // step,),
        in_specs=[IN_SMEM, IN_SMEM, w, w],
        out_specs=pl.BlockSpec((2, step, cols), lambda k: (0, k, 0)),
        name="masked_pair",
    )
    return pltpu.with_memory_space_constraint(pair, pltpu.VMEM)


def forward_own(hidden, pair, deps):
    rows, cols = hidden.shape[0], pair.shape[2]

    def body(h, w, out):
        for j in range(2):
            out[j] = jnp.dot(h[...], w[j], preferred_element_type=F32).astype(BF)

    return ordered(body, deps, [hidden, pair], shaped((2, rows, cols), BF), name="forward_own", pair=pair)


def forward_both(info, own, hidden, pair, deps):
    rows, cols = hidden.shape[0], pair.shape[2]

    def body(info_ref, o, h, w, out):
        x = info_ref[0]
        for j in range(2):
            part = jnp.dot(h[...], w[j], preferred_element_type=F32).astype(BF)
            out[jnp.where(x == 0, 3 - 2 * j, 2 - 2 * j)] = part
            out[jnp.where(x == 0, 2 * j, 1 + 2 * j)] = o[j]

    return ordered(
        body,
        deps,
        [info, own, hidden, pair],
        shaped((4, rows, cols), BF),
        in_specs=[IN_SMEM] + [IN_VMEM] * 3,
        name="forward_both",
        pair=pair,
    )


def cut(info, grads, deps):
    rows, cols = grads.shape
    half = cols // 2

    def body(info_ref, g, mine, theirs):
        x = info_ref[0]
        mine[...] = g[:, pl.ds(pl.multiple_of(x * half, half), half)]
        theirs[...] = g[:, pl.ds(pl.multiple_of((1 - x) * half, half), half)]

    out = jax.ShapeDtypeStruct((rows, half), BF)
    return ordered(body, deps, [info, grads], [out, out], in_specs=[IN_SMEM, IN_VMEM], name="cut")


def per_core(info, g0, g1, deps):
    rows, cols = g0.shape
    half = cols // 2

    def body(info_ref, a, b, mine, theirs):
        core = info_ref[1]
        for at, g in enumerate((a, b)):
            s = slice(at * rows, (at + 1) * rows)
            mine[s, :] = g[:, pl.ds(pl.multiple_of(core * half, half), half)]
            theirs[s, :] = g[:, pl.ds(pl.multiple_of((1 - core) * half, half), half)]

    out = jax.ShapeDtypeStruct((2 * rows, half), BF)
    return ordered(body, deps, [info, g0, g1], [out, out], in_specs=[IN_SMEM, IN_VMEM, IN_VMEM], name="per_core")


def back(grads, pair, first, width, dtype, deps, flops=1):
    step = 512
    cols = pair.shape[2]

    def body(g, w, out):
        for k in range(0, width, step):
            rows = slice(first + k, first + k + step)
            part = lax.dot_general(g[:, :cols], w[0, rows, :], COLS_CONTRACT, preferred_element_type=F32)
            part += lax.dot_general(g[:, cols:], w[1, rows, :], COLS_CONTRACT, preferred_element_type=F32)
            out[:, k : k + step] = part.astype(dtype)

    return ordered(body, deps, [grads, pair], shaped((grads.shape[0], width), dtype), name="back", pair=pair, flops=flops)


def relay(a, deps):
    def body(src, out):
        out[...] = src[...]

    return ordered(body, deps, [a], shaped(a.shape, a.dtype), name="relay")


def choose(info, own, received, deps):
    def body(info_ref, a, b, out):
        out[...] = jnp.where(info_ref[2] == 0, a[...], b[...])

    return ordered(
        body, deps, [info, own, received], shaped(own.shape, BF), in_specs=[IN_SMEM, IN_VMEM, IN_VMEM], name="choose"
    )


def hidden_grads(part, got, gate, up, first, made, deps):
    rows, width = got.shape
    unit = 512

    def body(p, r, gate_ref, up_ref, *refs):
        d_gate, d_up = refs[-2:]
        g, u = gate_ref[...].astype(F32), up_ref[...].astype(F32)
        s = jax.nn.sigmoid(g)
        d_hidden = p[...] + r[...].astype(F32)
        d_gate[...] = (d_hidden * u * s * (1.0 + g * (1.0 - s))).astype(BF)
        d_up[...] = (d_hidden * (g * s)).astype(BF)

    at = pl.BlockSpec((rows, unit), lambda k: (0, first // unit + k))
    return ordered(
        body,
        deps,
        [part, got, gate, up, *made],
        [shaped(gate.shape, BF)] * 2,
        grid=(width // unit,),
        in_specs=[at, pl.BlockSpec((rows, unit), lambda k: (0, k)), at, at] + [ANYWHERE] * len(made),
        out_specs=[at, at],
        aliases={4: 0, 5: 1} if made else None,
        name="hidden_grads",
    )


def weight_grad(info, mask, hidden, grads, deps):
    n = len(hidden)
    rows = sum(h.shape[0] for h in hidden)
    hid, cols = hidden[0].shape[1], grads[0].shape[1]
    step = 512

    def body(info_ref, mask_ref, *refs):
        hid_refs, grad_refs, (out, all_grads) = refs[:n], refs[n:-2], refs[-2:]

        @pl.when(pl.program_id(0) == 0)
        def _():
            at = 0
            for g in grad_refs:
                all_grads[at : at + g.shape[0], :] = g[...]
                at += g.shape[0]

        h = jnp.concatenate([r[...] for r in hid_refs], 0)
        total = lax.dot_general(h, all_grads[...], ROWS_CONTRACT, preferred_element_type=F32)
        row = pl.program_id(0) * (step // BLK)
        out[...] = kept(total, mask_ref, row, (2 * info_ref[0] + info_ref[1]) * (cols // BLK), 8)

    return ordered(
        body,
        deps,
        [info, mask, *hidden, *grads],
        shaped((hid, cols), F32),
        grid=(hid // step,),
        in_specs=[IN_SMEM, IN_SMEM]
        + [pl.BlockSpec((h.shape[0], step), lambda i: (0, i)) for h in hidden]
        + [pl.BlockSpec(g.shape, lambda i: (0, 0)) for g in grads],
        out_specs=pl.BlockSpec((step, cols), lambda i: (i, 0)),
        scratch=[pltpu.VMEM((rows, cols), BF)],
        name="weight_grad",
    )


def four_by_four(gate_pre, up_pre, down_weight, block_mask, grad_out):
    n_t = 4
    d, z = lax.axis_index("dp"), lax.axis_index("tensor")
    x, core = d // 2, d % 2
    q = jnp.where(x == 0, z, n_t - 1 - z)
    tokens, hid = gate_pre.shape
    info = jnp.stack([x, core, q]).astype(jnp.int32)

    def over_x(a):
        return lax.ppermute(a, "dp", [(i, i ^ 2) for i in range(4)])

    def over_core(a):
        return lax.ppermute(a, "dp", [(i, i ^ 1) for i in range(4)])

    def to_owner(a):
        perm = []
        for dd in range(4):
            line = [0, 1, 2, 3] if dd // 2 == 0 else [3, 2, 1, 0]
            perm.append((dd * n_t + line[1], (dd ^ 2) * n_t + line[1]))
            perm.append((dd * n_t + line[2], dd * n_t + line[1]))
            perm.append((dd * n_t + line[3], (dd ^ 2) * n_t + line[0]))
        return lax.ppermute(a, ("dp", "tensor"), perm)

    other = over_core(down_weight)
    full_grad = lax.all_gather(grad_out, "tensor", axis=1, tiled=True)
    h0 = hidden_of(gate_pre, up_pre, [])
    h1 = over_x(h0)
    h2 = over_core(h0)
    pair = masked_pair(info, block_mask, down_weight, other, [h0])
    o0 = forward_own(h0, pair, [h2])
    g0, gx = cut(info, full_grad, [o0])
    g1 = over_x(gx)
    o_all = forward_both(info, o0, h1, pair, [g0])
    out = lax.psum_scatter(o_all, "tensor", scatter_dimension=0, tiled=False)
    h3 = over_core(h1)
    part = back(g0, pair, 0, hid, F32, [o_all])
    parts = [(0, 3 * hid // 8), (3 * hid // 8, 3 * hid // 8), (3 * hid // 4, hid // 4)]
    last, got = part, []
    for first, width in parts:
        last = back(g1, pair, first, width, BF, [last], 6 * 10**10)
        got.append(over_x(last))
    g_own, g_theirs = per_core(info, g0, g1, [last])
    g_core = over_core(g_theirs)
    d_weight = weight_grad(info, block_mask, [h0, h1, h2, h3], [g_own, g_core], [])
    made, deps = [], [d_weight]
    for (first, _), g in zip(parts, got):
        made, deps = list(hidden_grads(part, g, gate_pre, up_pre, first, made, deps)), []
    done = relay(out, [d_weight])
    output = choose(info, done, to_owner(done), [made[0]])
    return (output, *made, d_weight)


def solution(mesh):
    fits = mesh.shape["dp"] == 4 and mesh.shape["tensor"] == 4
    return jax.shard_map(
        four_by_four if fits else any_mesh,
        mesh=mesh,
        in_specs=(
            P(("groups", "dp"), "tensor"),
            P(("groups", "dp"), "tensor"),
            P("tensor", "dp"),
            P("tensor", None),
            P(("groups", "dp"), "tensor"),
        ),
        out_specs=(
            P(("groups", "dp"), "tensor"),
            P(("groups", "dp"), "tensor"),
            P(("groups", "dp"), "tensor"),
            P(("groups", "tensor"), "dp"),
        ),
        check_vma=False,
    )
```

time: 474 us -> 167 us (0.35)
  waiting for transfers between devices: 325 us -> 51.2 us
  Pallas kernels: 0 us -> 71.9 us
  matrix products: 56.3 us -> 0 us
  blocking collectives: 29.3 us -> 0 us
  local copies, waits for them, and re-layouts: 42.3 us -> 18.7 us
  starting transfers between devices: 0.16 us -> 9.81 us
  other arithmetic: 6.87 us -> 0.08 us
    all_gather x3 -> x1, waiting for transfers between devices: 286 us -> 16.2 us  [four_by_four(): full_grad = lax.all_gather(grad_out, 'tensor', axis=1, tiled=True)]
    pallas_call x0 -> x16, Pallas kernels: none -> 71.9 us  [ordered(): pl.pallas_call(run, grid=grid, in_specs=in_specs + [ANYWHERE] * m, out_sp...]
    dot_general x3 -> x0, matrix products: 56.3 us -> none  [the longest x1 20 us: per_device(): lax.dot_general(full_grad, gathered, (((1,), (1,)), ((), ())), preferred_...]
    reduce_scatter x1, waiting for transfers between devices: 37.5 us -> 5.8 us  [four_by_four(): out = lax.psum_scatter(o_all, 'tensor', scatter_dimension=0, tiled=False)]
    all_to_all x1 -> x0, blocking collectives: 29.3 us -> none  [per_device(): lax.all_to_all(full_grad, 'dp', split_axis=1, concat_axis=0, tiled=True)]
    ppermute x0 -> x10, waiting for transfers between devices: none -> 29 us  [the longest x5 23.8 us: over_x(): return lax.ppermute(a, 'dp', [(i, i ^ 2) for i in range(4)])]
    broadcast_in_dim x4 -> x0, local copies, waits for them, and re-layouts: 22.7 us -> none  [expand_mask(): widened = jnp.repeat(jnp.repeat(small_mask, BLK, axis=0), BLK, axis=1)]
    ppermute x0 -> x10, starting transfers between devices: none -> 9.73 us  [the longest x5 7.49 us: over_x(): return lax.ppermute(a, 'dp', [(i, i ^ 2) for i in range(4)])]
  transfers between devices with their start and end apart: 4 -> 12, of which waited for: 4 -> 5; matrix products, arithmetic and copies ran while one was open for 7% -> 0% of each run, Pallas kernels for 0% -> 43%
where the time goes in v2:
time: 167 us; the launch traced here: 166 us
  Pallas kernels  71.9 us (43%)
  waiting for transfers between devices  51.2 us (31%)
  local copies, waits for them, and re-layouts  18.7 us (11%)
  between operations  14.1 us (8%)
  starting transfers between devices  9.81 us (6%)
    pallas_call x16, Pallas kernels, ordered(): pl.pallas_call(run, grid=grid, in_specs=in_specs + [ANYWHERE] * m, out_sp...  71.9 us
    ppermute x5, waiting for transfers between devices, over_x(): return lax.ppermute(a, 'dp', [(i, i ^ 2) for i in range(4)])  23.8 us
    unnamed x12, local copies, waits for them, and re-layouts  18.7 us
    all_gather x1, waiting for transfers between devices, four_by_four(): full_grad = lax.all_gather(grad_out, 'tensor', axis=1, tiled=True)  16.2 us
    ppermute x5, starting transfers between devices, over_x(): return lax.ppermute(a, 'dp', [(i, i ^ 2) for i in range(4)])  7.49 us
    reduce_scatter x1, waiting for transfers between devices, four_by_four(): out = lax.psum_scatter(o_all, 'tensor', scatter_dimension=0, tiled=False)  5.8 us
    ppermute x4, waiting for transfers between devices, over_core(): return lax.ppermute(a, 'dp', [(i, i ^ 1) for i in range(4)])  5.22 us
  transfers between devices with their start and end apart: 12, of which 5 were waited for; matrix products, arithmetic and copies ran while one was open for 0% of the time, Pallas kernels for 43%

profile of v2, /device:TPU:0, one launch (start us, length us, event | category | flops | bytes accessed | tf_op | source)
XLA Modules:
  0.0 165.9 jit_solution(5679659226090506798)
XLA Ops:
  7.2 0.5 collective-permute-start
  8.0 4.7 %hidden.1.refs_4_.refs_0_.refs_2_ = bf16[256,4096]{1,0:T(8,128)(2,1)} custom-call(bf16[256,4096]{1,0:T(8,128)(2,1)} %refs_2_.7, bf16[256,4096]{1,0:T(8,128)(2,1)} %refs_3_.5), custom_call_target="tpu_custom_call" | custom-call | flops 1 | bytes 1 | tf_op jit(solution)/shard_map/hidden/pallas_call | solution.py:84
  13.1 2.5 %collective-permute-start.2 = (bf16[256,4096]{1,0:T(8,128)(2,1)}, bf16[256,4096]{1,0:T(8,128)(2,1)}, u32[]{:S(2)}, u32[]{:S(2)}) collective-permute-start(bf16[256,4096]{1,0:T(8,128)(2,1)} %hidden.1.refs_4_.refs_0_.refs_2_), channel_id=1, source_target_pairs={{0,8},{4,12},{8,0},{12,4},{1,9},{5,13},{9,1},{13,5},{2,10},{6,14},... | collective-permute-start | bytes 6291464 | tf_op jit(solution)/shard_map/ppermute | solution.py:314
  15.6 5.2 %collective-permute-done.refs_3_ = bf16[4096,1024]{1,0:T(8,128)(2,1)} collective-permute-done((bf16[4096,1024]{1,0:T(8,128)(2,1)}, bf16[4096,1024]{1,0:T(8,128)(2,1)}, u32[]{:S(2)}, u32[]{:S(2)}) %collective-permute-start) | collective-permute-done | bytes 8388640 | tf_op jit(solution)/shard_map/ppermute | solution.py:317
  20.9 8.9 %masked_pair.1.refs_1_.refs_3_ = bf16[2,4096,1024]{2,1,0:T(8,128)(2,1)S(1)} custom-call(s32[3]{0:T(128)S(1)} %pad_add_fusion.refs_0_, s32[32,32]{1,0:T(8,128)S(1)} %copy-done.4, bf16[4096,1024]{1,0:T(8,128)(2,1)} %refs_2_.4, bf16[4096,1024]{1,0:T(8,128)(2,1)} %collective-permute-done.refs_3_, bf16[256,4096]{1,0:T(8,128)(2,1)} %hidden.1.refs_4_.refs_0_.refs_2_), custom_call_target="tpu_custom_call" | custom-call | flops 1 | bytes 1 | tf_op jit(solution)/shard_map/masked_pair/pallas_call | solution.py:84
  29.8 6.1 %forward_own.1.refs_2_.refs_1_ = bf16[2,256,1024]{2,1,0:T(8,128)(2,1)S(1)} custom-call(bf16[256,4096]{1,0:T(8,128)(2,1)} %hidden.1.refs_4_.refs_0_.refs_2_, bf16[2,4096,1024]{2,1,0:T(8,128)(2,1)S(1)} %masked_pair.1.refs_1_.refs_3_, bf16[256,4096]{1,0:T(8,128)(2,1)} %collective-permute-done.1.refs_2_.refs_4_), custom_call_target="tpu_custom_call" | custom-call | flops 1 | bytes 1 | tf_op jit(solution)/shard_map/forward_own/pallas_call | solution.py:84
  35.9 6.2 %copy-done = bf16[2,4096,1024]{2,1,0:T(8,128)(2,1)} copy-done((bf16[2,4096,1024]{2,1,0:T(8,128)(2,1)}, bf16[2,4096,1024]{2,1,0:T(8,128)(2,1)S(1)}, u32[]{:S(2)}) %copy-start) | copy-done | bytes 16777240
  42.1 16.2 %all-gather.2.cloned.1.call-done.refs_1_ = bf16[256,4096]{1,0:T(8,128)(2,1)} async-done(((bf16[256,1024]{1,0:T(8,128)(2,1)}), bf16[256,4096]{1,0:T(8,128)(2,1)}) %all-gather.2.cloned.1.call-update) | async-done | bytes 2097168 | tf_op jit(solution)/shard_map/all_gather | solution.py:329
  58.2 2.7 %cut.1 = (bf16[256,2048]{1,0:T(8,128)(2,1)S(1)}, bf16[256,2048]{1,0:T(8,128)(2,1)}) custom-call(s32[3]{0:T(128)S(1)} %pad_add_fusion.refs_0_, bf16[256,4096]{1,0:T(8,128)(2,1)} %all-gather.2.cloned.1.call-done.refs_1_, bf16[2,256,1024]{2,1,0:T(8,128)(2,1)S(1)} %forward_own.1.refs_2_.refs_1_), custom_call_target="tpu_custom_call" | custom-call | flops 1 | bytes 1 | tf_op jit(solution)/shard_map/cut/pallas_call | solution.py:84
  61.0 1.5 collective-permute-start.4
  62.4 5.8 %copy-done.1 = bf16[2,4096,1024]{2,1,0:T(8,128)(2,1)S(1)} copy-done((bf16[2,4096,1024]{2,1,0:T(8,128)(2,1)S(1)}, bf16[2,4096,1024]{2,1,0:T(8,128)(2,1)}, u32[]{:S(2)}) %copy-start.1) | copy-done | bytes 16777240
  68.2 7.4 %forward_both.1.refs_2_ = bf16[4,256,1024]{2,1,0:T(8,128)(2,1)} custom-call(s32[3]{0:T(128)S(1)} %pad_add_fusion.refs_0_, bf16[2,256,1024]{2,1,0:T(8,128)(2,1)S(1)} %forward_own.1.refs_2_.refs_1_, bf16[256,4096]{1,0:T(8,128)(2,1)} %collective-permute-done.2.refs_2_.refs_3_, bf16[2,4096,1024]{2,1,0:T(8,128)(2,1)S(1)} %copy-done.1, ...), custom_call_target="tpu_custom_call" | custom-call | flops 1 | bytes 1 | tf_op jit(solution)/shard_map/forward_both/pallas_call | solution.py:84
  75.7 5.8 %copy-done.2 = bf16[2,4096,1024]{2,1,0:T(8,128)(2,1)S(1)} copy-done((bf16[2,4096,1024]{2,1,0:T(8,128)(2,1)S(1)}, bf16[2,4096,1024]{2,1,0:T(8,128)(2,1)}, u32[]{:S(2)}) %copy-start.2) | copy-done | bytes 16777240
  81.4 6.5 %back.4.refs_2_.refs_0_ = f32[256,4096]{1,0:T(8,128)} custom-call(bf16[256,2048]{1,0:T(8,128)(2,1)S(1)} %get-tuple-element.14.refs_4_.refs_0_.refs_1_, bf16[2,4096,1024]{2,1,0:T(8,128)(2,1)S(1)} %copy-done.2, bf16[4,256,1024]{2,1,0:T(8,128)(2,1)} %forward_both.1.refs_2_), custom_call_target="tpu_custom_call" | custom-call | flops 1 | bytes 1 | tf_op jit(solution)/shard_map/back/pallas_call | solution.py:84
  87.9 2.7 %back.5.refs_2_ = bf16[256,1536]{1,0:T(8,128)(2,1)} custom-call(bf16[256,2048]{1,0:T(8,128)(2,1)S(1)} %collective-permute-done.4.refs_0_.refs_2_, bf16[2,4096,1024]{2,1,0:T(8,128)(2,1)S(1)} %copy-done.2, f32[256,4096]{1,0:T(8,128)} %back.4.refs_2_.refs_0_), custom_call_target="tpu_custom_call" | custom-call | flops 60000002048 | bytes 1 | tf_op jit(solution)/shard_map/back/pallas_call | solution.py:84
  90.7 2.9 %back.6.refs_2_ = bf16[256,1536]{1,0:T(8,128)(2,1)} custom-call(bf16[256,2048]{1,0:T(8,128)(2,1)S(1)} %collective-permute-done.4.refs_0_.refs_2_, bf16[2,4096,1024]{2,1,0:T(8,128)(2,1)S(1)} %copy-done.2, bf16[256,1536]{1,0:T(8,128)(2,1)} %back.5.refs_2_), custom_call_target="tpu_custom_call" | custom-call | flops 60000002048 | bytes 1 | tf_op jit(solution)/shard_map/back/pallas_call | solution.py:84
  93.6 2.1 %back.7.refs_3_ = bf16[256,1024]{1,0:T(8,128)(2,1)} custom-call(bf16[256,2048]{1,0:T(8,128)(2,1)S(1)} %collective-permute-done.4.refs_0_.refs_2_, bf16[2,4096,1024]{2,1,0:T(8,128)(2,1)S(1)} %copy-done.2, bf16[256,1536]{1,0:T(8,128)(2,1)} %back.6.refs_2_), custom_call_target="tpu_custom_call" | custom-call | flops 60000002048 | bytes 1 | tf_op jit(solution)/shard_map/back/pallas_call | solution.py:84
  95.7 0.7 per_core.1
  96.3 0.6 collective-permute-start.5
  96.9 1.5 collective-permute-start.9
  98.4 0.5 collective-permute-start.8
  98.9 1.5 collective-permute-start.7
  100.5 15.2 %weight_grad.1.refs_1_.refs_4_ = f32[4096,1024]{1,0:T(8,128)} custom-call(s32[3]{0:T(128)S(1)} %pad_add_fusion.refs_0_, s32[32,32]{1,0:T(8,128)S(1)} %copy-done.5, bf16[256,4096]{1,0:T(8,128)(2,1)} %hidden.1.refs_4_.refs_0_.refs_2_, bf16[256,4096]{1,0:T(8,128)(2,1)} %collective-permute-done.2.refs_2_.refs_3_, ...), custom_call_target="tpu_custom_call" | custom-call | flops 1 | bytes 1 | tf_op jit(solution)/shard_map/weight_grad/pallas_call | solution.py:84
  115.7 5.8 %reduce-scatter.2.cloned.1.call-done = bf16[1,256,1024]{2,1,0:T(8,128)(2,1)} async-done(((bf16[4,256,1024]{2,1,0:T(8,128)(2,1)}), bf16[1,256,1024]{2,1,0:T(8,128)(2,1)}) %reduce-scatter.2.cloned.1.call-update) | async-done | bytes 524304 | tf_op jit(solution)/shard_map/reduce_scatter | solution.py:338
  121.5 1.0 copy-done.3
  122.6 0.7 collective-permute-start.6
  123.3 4.0 %hidden_grads.3 = (bf16[256,4096]{1,0:T(8,128)(2,1)}, bf16[256,4096]{1,0:T(8,128)(2,1)}) custom-call(f32[256,4096]{1,0:T(8,128)} %back.4.refs_2_.refs_0_, bf16[256,1536]{1,0:T(8,128)(2,1)S(1)} %collective-permute-done.9.refs_1_, bf16[256,4096]{1,0:T(8,128)(2,1)} %refs_2_.7, bf16[256,4096]{1,0:T(8,128)(2,1)} %refs_3_.5, f32[4096,1024]{1,0:T(8,128)} %weight_grad.1.refs_1_.refs_4_), custom_call_target="tpu_custom_call" | custom-call | flops 1 | bytes 1 | tf_op jit(solution)/shard_map/hidden_grads/pallas_call | solution.py:84
  127.3 17.5 %collective-permute-done.8.refs_1_ = bf16[256,1536]{1,0:T(8,128)(2,1)S(1)} collective-permute-done((bf16[256,1536]{1,0:T(8,128)(2,1)}, bf16[256,1536]{1,0:T(8,128)(2,1)S(1)}, u32[]{:S(2)}, u32[]{:S(2)}) %collective-permute-start.8) | collective-permute-done | bytes 786464 | tf_op jit(solution)/shard_map/ppermute | solution.py:314
  144.8 4.0 %hidden_grads.4 = (bf16[256,4096]{1,0:T(8,128)(2,1)}, bf16[256,4096]{1,0:T(8,128)(2,1)}) custom-call(f32[256,4096]{1,0:T(8,128)} %back.4.refs_2_.refs_0_, bf16[256,1536]{1,0:T(8,128)(2,1)S(1)} %collective-permute-done.8.refs_1_, bf16[256,4096]{1,0:T(8,128)(2,1)} %refs_2_.7, bf16[256,4096]{1,0:T(8,128)(2,1)} %refs_3_.5, ...), custom_call_target="tpu_custom_call", output_to_operand_aliasing={{0}: (4, {}), {1}: (5, {})} | custom-call | flops 1 | bytes 1 | tf_op jit(solution)/shard_map/hidden_grads/pallas_call | solution.py:84
  148.8 6.4 %collective-permute-done.7.refs_1_ = bf16[256,1024]{1,0:T(8,128)(2,1)S(1)} collective-permute-done((bf16[256,1024]{1,0:T(8,128)(2,1)}, bf16[256,1024]{1,0:T(8,128)(2,1)S(1)}, u32[]{:S(2)}, u32[]{:S(2)}) %collective-permute-start.7) | collective-permute-done | bytes 524320 | tf_op jit(solution)/shard_map/ppermute | solution.py:314
  155.1 2.5 %hidden_grads.5 = (bf16[256,4096]{1,0:T(8,128)(2,1)}, bf16[256,4096]{1,0:T(8,128)(2,1)}) custom-call(f32[256,4096]{1,0:T(8,128)} %back.4.refs_2_.refs_0_, bf16[256,1024]{1,0:T(8,128)(2,1)S(1)} %collective-permute-done.7.refs_1_, bf16[256,4096]{1,0:T(8,128)(2,1)} %refs_2_.7, bf16[256,4096]{1,0:T(8,128)(2,1)} %refs_3_.5, ...), custom_call_target="tpu_custom_call", output_to_operand_aliasing={{0}: (4, {}), {1}: (5, {})} | custom-call | flops 1 | bytes 1 | tf_op jit(solution)/shard_map/hidden_grads/pallas_call | solution.py:84
  157.7 1.4 choose.1
  (23 shorter events, 0.9 us)
Async XLA Ops:
  7.2 51.1 %all-gather.2.cloned.1.call-start = ((), (), s32[]{:S(2)}) async-start(), calls=%async_computation.1 | async-start | bytes 2621440 | tf_op jit(solution)/shard_map/all_gather | solution.py:329
  7.2 13.6 %collective-permute-start = (bf16[4096,1024]{1,0:T(8,128)(2,1)}, bf16[4096,1024]{1,0:T(8,128)(2,1)}, u32[]{:S(2)}, u32[]{:S(2)}) collective-permute-start(bf16[4096,1024]{1,0:T(8,128)(2,1)} %refs_2_.4), channel_id=1, source_target_pairs={{0,4},{4,0},{8,12},{12,8},{1,5},{5,1},{9,13},{13,9},{2,6},{6,2},{1... | collective-permute-start | bytes 25165832 | tf_op jit(solution)/shard_map/ppermute | solution.py:317
  7.9 13.0 %copy-start.4 = (s32[32,32]{1,0:T(8,128)S(1)}, s32[32,32]{1,0:T(8,128)}, u32[]{:S(2)}) copy-start(s32[32,32]{1,0:T(8,128)} %refs_1_.5) | copy-start | bytes 12292
  7.9 113.6 %reduce-scatter.2.cloned.1.call-start = ((), (), s32[]{:S(2)}) async-start(), calls=%async_computation.2 | async-start | bytes 2621440 | tf_op jit(solution)/shard_map/reduce_scatter | solution.py:338
  12.6 17.2 %collective-permute-start.1 = (bf16[256,4096]{1,0:T(8,128)(2,1)}, bf16[256,4096]{1,0:T(8,128)(2,1)}, u32[]{:S(2)}, u32[]{:S(2)}) collective-permute-start(bf16[256,4096]{1,0:T(8,128)(2,1)} %hidden.1.refs_4_.refs_0_.refs_2_), channel_id=1, source_target_pairs={{0,4},{4,0},{8,12},{12,8},{1,5},{5,1},{9,13},{13,9},{2,6},{6,2},{1... | collective-permute-start | bytes 6291464 | tf_op jit(solution)/shard_map/ppermute | solution.py:317
  13.1 49.3 %collective-permute-start.2 = (bf16[256,4096]{1,0:T(8,128)(2,1)}, bf16[256,4096]{1,0:T(8,128)(2,1)}, u32[]{:S(2)}, u32[]{:S(2)}) collective-permute-start(bf16[256,4096]{1,0:T(8,128)(2,1)} %hidden.1.refs_4_.refs_0_.refs_2_), channel_id=1, source_target_pairs={{0,8},{4,12},{8,0},{12,4},{1,9},{5,13},{9,1},{13,5},{2,10},{6,14},... | collective-permute-start | bytes 6291464 | tf_op jit(solution)/shard_map/ppermute | solution.py:314
  35.9 6.2 %copy-start = (bf16[2,4096,1024]{2,1,0:T(8,128)(2,1)}, bf16[2,4096,1024]{2,1,0:T(8,128)(2,1)S(1)}, u32[]{:S(2)}) copy-start(bf16[2,4096,1024]{2,1,0:T(8,128)(2,1)S(1)} %masked_pair.1.refs_1_.refs_3_) | copy-start | bytes 50331652
  61.0 27.0 %collective-permute-start.4 = (bf16[256,2048]{1,0:T(8,128)(2,1)}, bf16[256,2048]{1,0:T(8,128)(2,1)S(1)}, u32[]{:S(2)}, u32[]{:S(2)}) collective-permute-start(bf16[256,2048]{1,0:T(8,128)(2,1)} %get-tuple-element.15), channel_id=1, source_target_pairs={{0,8},{4,12},{8,0},{12,4},{1,9},{5,13},{9,1},{13,5},{2,10},{6,14},... | collective-permute-start | bytes 3145736 | tf_op jit(solution)/shard_map/ppermute | solution.py:314
  62.4 38.0 %collective-permute-start.3 = (bf16[256,4096]{1,0:T(8,128)(2,1)}, bf16[256,4096]{1,0:T(8,128)(2,1)}, u32[]{:S(2)}, u32[]{:S(2)}) collective-permute-start(bf16[256,4096]{1,0:T(8,128)(2,1)} %collective-permute-done.2.refs_2_.refs_3_), channel_id=1, source_target_pairs={{0,4},{4,0},{8,12},{12,8},{1,5},{5,1},{9,13},{13,9},{2,6},{6,2},{1... | collective-permute-start | bytes 6291464 | tf_op jit(solution)/shard_map/ppermute | solution.py:317
  62.4 5.8 %copy-start.1 = (bf16[2,4096,1024]{2,1,0:T(8,128)(2,1)S(1)}, bf16[2,4096,1024]{2,1,0:T(8,128)(2,1)}, u32[]{:S(2)}) copy-start(bf16[2,4096,1024]{2,1,0:T(8,128)(2,1)} %copy-done) | copy-start | bytes 50331652
  75.6 5.8 %copy-start.2 = (bf16[2,4096,1024]{2,1,0:T(8,128)(2,1)S(1)}, bf16[2,4096,1024]{2,1,0:T(8,128)(2,1)}, u32[]{:S(2)}) copy-start(bf16[2,4096,1024]{2,1,0:T(8,128)(2,1)} %copy-done) | copy-start | bytes 50331652
  95.7 4.8 %copy-start.5 = (s32[32,32]{1,0:T(8,128)S(1)}, s32[32,32]{1,0:T(8,128)}, u32[]{:S(2)}) copy-start(s32[32,32]{1,0:T(8,128)} %refs_1_.5) | copy-start | bytes 12292
  96.3 4.1 %collective-permute-start.5 = (bf16[512,1024]{1,0:T(8,128)(2,1)S(1)}, bf16[512,1024]{1,0:T(8,128)(2,1)S(1)}, u32[]{:S(2)}, u32[]{:S(2)}) collective-permute-start(bf16[512,1024]{1,0:T(8,128)(2,1)S(1)} %get-tuple-element.17), channel_id=1, source_target_pairs={{0,4},{4,0},{8,12},{12,8},{1,5},{5,1},{9,13},{13,9},{2,6},{6,2},{1... | collective-permute-start | bytes 3145736 | tf_op jit(solution)/shard_map/ppermute | solution.py:317
  96.9 26.3 %collective-permute-start.9 = (bf16[256,1536]{1,0:T(8,128)(2,1)}, bf16[256,1536]{1,0:T(8,128)(2,1)S(1)}, u32[]{:S(2)}, u32[]{:S(2)}) collective-permute-start(bf16[256,1536]{1,0:T(8,128)(2,1)} %back.5.refs_2_), channel_id=1, source_target_pairs={{0,8},{4,12},{8,0},{12,4},{1,9},{5,13},{9,1},{13,5},{2,10},{6,14},... | collective-permute-start | bytes 2359304 | tf_op jit(solution)/shard_map/ppermute | solution.py:314
  98.4 46.3 %collective-permute-start.8 = (bf16[256,1536]{1,0:T(8,128)(2,1)}, bf16[256,1536]{1,0:T(8,128)(2,1)S(1)}, u32[]{:S(2)}, u32[]{:S(2)}) collective-permute-start(bf16[256,1536]{1,0:T(8,128)(2,1)} %back.6.refs_2_), channel_id=1, source_target_pairs={{0,8},{4,12},{8,0},{12,4},{1,9},{5,13},{9,1},{13,5},{2,10},{6,14},... | collective-permute-start | bytes 2359304 | tf_op jit(solution)/shard_map/ppermute | solution.py:314
  98.9 56.2 %collective-permute-start.7 = (bf16[256,1024]{1,0:T(8,128)(2,1)}, bf16[256,1024]{1,0:T(8,128)(2,1)S(1)}, u32[]{:S(2)}, u32[]{:S(2)}) collective-permute-start(bf16[256,1024]{1,0:T(8,128)(2,1)} %back.7.refs_3_), channel_id=1, source_target_pairs={{0,8},{4,12},{8,0},{12,4},{1,9},{5,13},{9,1},{13,5},{2,10},{6,14},... | collective-permute-start | bytes 1572872 | tf_op jit(solution)/shard_map/ppermute | solution.py:314
  121.5 1.0 copy-start.3
  122.6 35.1 %collective-permute-start.6 = (bf16[256,1024]{1,0:T(8,128)(2,1)S(1)}, bf16[256,1024]{1,0:T(8,128)(2,1)S(1)}, u32[]{:S(2)}, u32[]{:S(2)}) collective-permute-start(bf16[256,1024]{1,0:T(8,128)(2,1)S(1)} %relay.1.refs_1_), channel_id=1, source_target_pairs={{1,9},{2,1},{3,8},{5,13},{6,5},{7,12},{10,2},{9,10},{8,3},{14,6},{... | collective-permute-start | bytes 1572872 | tf_op jit(solution)/shard_map/ppermute | solution.py:326
Sparse Core Ops, SparseCore 0:
  9.6 48.6 all-gather.1
  75.8 45.6 reduce-scatter.1

commit v3 on v2

--- a/solution.py
+++ b/solution.py
@@ -164,7 +164,8 @@
 def forward_both(info, own, hidden, pair, deps):
     rows, cols = hidden.shape[0], pair.shape[2]
 
-    def body(info_ref, o, h, w, out):
+    def body(info_ref, o, h, w, out, passed):
+        del passed
         x = info_ref[0]
         for j in range(2):
             part = jnp.dot(h[...], w[j], preferred_element_type=F32).astype(BF)
@@ -175,8 +176,10 @@
         body,
         deps,
         [info, own, hidden, pair],
-        shaped((4, rows, cols), BF),
+        [shaped((4, rows, cols), BF), shaped(hidden.shape, BF)],
         in_specs=[IN_SMEM] + [IN_VMEM] * 3,
+        out_specs=[IN_VMEM, ANYWHERE],
+        aliases={2: 1},
         name="forward_both",
         pair=pair,
     )
@@ -195,19 +198,17 @@
     return ordered(body, deps, [info, grads], [out, out], in_specs=[IN_SMEM, IN_VMEM], name="cut")
 
 
-def per_core(info, g0, g1, deps):
-    rows, cols = g0.shape
+def per_core(info, grads, deps):
+    rows, cols = grads.shape
     half = cols // 2
 
-    def body(info_ref, a, b, mine, theirs):
+    def body(info_ref, g, mine, theirs):
         core = info_ref[1]
-        for at, g in enumerate((a, b)):
-            s = slice(at * rows, (at + 1) * rows)
-            mine[s, :] = g[:, pl.ds(pl.multiple_of(core * half, half), half)]
-            theirs[s, :] = g[:, pl.ds(pl.multiple_of((1 - core) * half, half), half)]
-
-    out = jax.ShapeDtypeStruct((2 * rows, half), BF)
-    return ordered(body, deps, [info, g0, g1], [out, out], in_specs=[IN_SMEM, IN_VMEM, IN_VMEM], name="per_core")
+        mine[...] = g[:, pl.ds(pl.multiple_of(core * half, half), half)]
+        theirs[...] = g[:, pl.ds(pl.multiple_of((1 - core) * half, half), half)]
+
+    out = jax.ShapeDtypeStruct((rows, half), BF)
+    return ordered(body, deps, [info, grads], [out, out], in_specs=[IN_SMEM, IN_VMEM], name="per_core")
 
 
 def back(grads, pair, first, width, dtype, deps, flops=1):
@@ -240,7 +241,7 @@
     )
 
 
-def hidden_grads(part, got, gate, up, first, made, deps):
+def hidden_grads(part, part_first, got, gate, up, first, made, deps):
     rows, width = got.shape
     unit = 512
 
@@ -253,13 +254,14 @@
         d_up[...] = (d_hidden * (g * s)).astype(BF)
 
     at = pl.BlockSpec((rows, unit), lambda k: (0, first // unit + k))
+    part_at = pl.BlockSpec((rows, unit), lambda k: (0, (first - part_first) // unit + k))
     return ordered(
         body,
         deps,
         [part, got, gate, up, *made],
         [shaped(gate.shape, BF)] * 2,
         grid=(width // unit,),
-        in_specs=[at, pl.BlockSpec((rows, unit), lambda k: (0, k)), at, at] + [ANYWHERE] * len(made),
+        in_specs=[part_at, pl.BlockSpec((rows, unit), lambda k: (0, k)), at, at] + [ANYWHERE] * len(made),
         out_specs=[at, at],
         aliases={4: 0, 5: 1} if made else None,
         name="hidden_grads",
@@ -334,21 +336,25 @@
     o0 = forward_own(h0, pair, [h2])
     g0, gx = cut(info, full_grad, [o0])
     g1 = over_x(gx)
-    o_all = forward_both(info, o0, h1, pair, [g0])
+    o_all, h1 = forward_both(info, o0, h1, pair, [g0])
     out = lax.psum_scatter(o_all, "tensor", scatter_dimension=0, tiled=False)
     h3 = over_core(h1)
-    part = back(g0, pair, 0, hid, F32, [o_all])
-    parts = [(0, 3 * hid // 8), (3 * hid // 8, 3 * hid // 8), (3 * hid // 4, hid // 4)]
-    last, got = part, []
-    for first, width in parts:
-        last = back(g1, pair, first, width, BF, [last], 6 * 10**10)
+    g0_own, g0_theirs = per_core(info, g0, [o_all])
+    parts = [(0, 5 * hid // 8), (5 * hid // 8, hid // 4), (7 * hid // 8, hid // 8)]
+    cut_at = parts[1][0]
+    own_part = [back(g0, pair, 0, cut_at, F32, [g0_own])]
+    last, got = own_part[0], []
+    for i, (first, width) in enumerate(parts):
+        last = back(g1, pair, first, width, BF, [last], 2 * 10**11 if i == 0 else 1)
         got.append(over_x(last))
-    g_own, g_theirs = per_core(info, g0, g1, [last])
-    g_core = over_core(g_theirs)
-    d_weight = weight_grad(info, block_mask, [h0, h1, h2, h3], [g_own, g_core], [])
+    g1_own, g1_theirs = per_core(info, g1, [last])
+    own_part.append(back(g0, pair, cut_at, hid - cut_at, F32, [g1_own]))
+    g_core = [over_core(g0_theirs), over_core(g1_theirs)]
+    d_weight = weight_grad(info, block_mask, [h0, h1, h2, h3], [g0_own, g1_own, *g_core], [own_part[1]])
     made, deps = [], [d_weight]
     for (first, _), g in zip(parts, got):
-        made, deps = list(hidden_grads(part, g, gate_pre, up_pre, first, made, deps)), []
+        own, own_first = (own_part[0], 0) if first < cut_at else (own_part[1], cut_at)
+        made, deps = list(hidden_grads(own, own_first, g, gate_pre, up_pre, first, made, deps)), []
     done = relay(out, [d_weight])
     output = choose(info, done, to_owner(done), [made[0]])
     return (output, *made, d_weight)

time: 167 us -> 160 us (0.958)
  waiting for transfers between devices: 51.2 us -> 39.4 us
  starting transfers between devices: 9.81 us -> 12.7 us
  local copies, waits for them, and re-layouts: 18.7 us -> 20.9 us
    ppermute x5, waiting for transfers between devices: 23.8 us -> 13 us  [over_x(): return lax.ppermute(a, 'dp', [(i, i ^ 2) for i in range(4)])]
    ppermute x5, starting transfers between devices: 7.49 us -> 10.2 us  [over_x(): return lax.ppermute(a, 'dp', [(i, i ^ 2) for i in range(4)])]
    unnamed x12 -> x20, local copies, waits for them, and re-layouts: 18.7 us -> 20.9 us
    pallas_call x16 -> x18, Pallas kernels: 71.9 us -> 72.4 us  [ordered(): pl.pallas_call(run, grid=grid, in_specs=in_specs + [ANYWHERE] * m, out_sp...]
    ppermute x4 -> x5, waiting for transfers between devices: 5.22 us -> 5.22 us  [over_core(): return lax.ppermute(a, 'dp', [(i, i ^ 1) for i in range(4)])]
  transfers between devices with their start and end apart: 12 -> 13, of which waited for: 5 -> 5; matrix products, arithmetic and copies ran while one was open for 0% -> 0% of each run, Pallas kernels for 43% -> 45%
where the time goes in v3:
time: 160 us
  Pallas kernels  72.4 us (45%)
  waiting for transfers between devices  39.4 us (25%)
  local copies, waits for them, and re-layouts  20.9 us (13%)
  between operations  14.2 us (9%)
  starting transfers between devices  12.7 us (8%)
    pallas_call x18, Pallas kernels, ordered(): pl.pallas_call(run, grid=grid, in_specs=in_specs + [ANYWHERE] * m, out_sp...  72.4 us
    unnamed x20, local copies, waits for them, and re-layouts  20.9 us
    all_gather x1, waiting for transfers between devices, four_by_four(): full_grad = lax.all_gather(grad_out, 'tensor', axis=1, tiled=True)  16 us
    ppermute x5, waiting for transfers between devices, over_x(): return lax.ppermute(a, 'dp', [(i, i ^ 2) for i in range(4)])  13 us
    ppermute x5, starting transfers between devices, over_x(): return lax.ppermute(a, 'dp', [(i, i ^ 2) for i in range(4)])  10.2 us
    ppermute x5, waiting for transfers between devices, over_core(): return lax.ppermute(a, 'dp', [(i, i ^ 1) for i in range(4)])  5.22 us
    reduce_scatter x1, waiting for transfers between devices, four_by_four(): out = lax.psum_scatter(o_all, 'tensor', scatter_dimension=0, tiled=False)  4.94 us
  transfers between devices with their start and end apart: 13, of which 5 were waited for; matrix products, arithmetic and copies ran while one was open for 0% of the time, Pallas kernels for 45%

profile of v3, /device:TPU:0, one launch (start us, length us, event | category | flops | bytes accessed | tf_op | source)
XLA Modules:
  0.0 159.5 jit_solution(16290867037517407689)
XLA Ops:
  8.0 4.7 %hidden.1.refs_4_.refs_0_.refs_2_ = bf16[256,4096]{1,0:T(8,128)(2,1)} custom-call(bf16[256,4096]{1,0:T(8,128)(2,1)} %refs_2_.7, bf16[256,4096]{1,0:T(8,128)(2,1)} %refs_3_.5), custom_call_target="tpu_custom_call" | custom-call | flops 1 | bytes 1 | tf_op jit(solution)/shard_map/hidden/pallas_call | solution.py:84
  13.1 2.5 %collective-permute-start.2 = (bf16[256,4096]{1,0:T(8,128)(2,1)}, bf16[256,4096]{1,0:T(8,128)(2,1)}, u32[]{:S(2)}, u32[]{:S(2)}) collective-permute-start(bf16[256,4096]{1,0:T(8,128)(2,1)} %hidden.1.refs_4_.refs_0_.refs_2_), channel_id=1, source_target_pairs={{0,8},{4,12},{8,0},{12,4},{1,9},{5,13},{9,1},{13,5},{2,10},{6,14},... | collective-permute-start | bytes 6291464 | tf_op jit(solution)/shard_map/ppermute | solution.py:316
  15.6 5.2 %collective-permute-done.refs_3_ = bf16[4096,1024]{1,0:T(8,128)(2,1)} collective-permute-done((bf16[4096,1024]{1,0:T(8,128)(2,1)}, bf16[4096,1024]{1,0:T(8,128)(2,1)}, u32[]{:S(2)}, u32[]{:S(2)}) %collective-permute-start) | collective-permute-done | bytes 8388640 | tf_op jit(solution)/shard_map/ppermute | solution.py:319
  20.9 9.0 %masked_pair.1.refs_1_.refs_3_ = bf16[2,4096,1024]{2,1,0:T(8,128)(2,1)S(1)} custom-call(s32[3]{0:T(128)S(1)} %pad_add_fusion.refs_0_, s32[32,32]{1,0:T(8,128)S(1)} %copy-done.4, bf16[4096,1024]{1,0:T(8,128)(2,1)} %refs_2_.4, bf16[4096,1024]{1,0:T(8,128)(2,1)} %collective-permute-done.refs_3_, bf16[256,4096]{1,0:T(8,128)(2,1)} %hidden.1.refs_4_.refs_0_.refs_2_), custom_call_target="tpu_custom_call" | custom-call | flops 1 | bytes 1 | tf_op jit(solution)/shard_map/masked_pair/pallas_call | solution.py:84
  29.8 6.2 %forward_own.1.refs_2_.refs_1_ = bf16[2,256,1024]{2,1,0:T(8,128)(2,1)S(1)} custom-call(bf16[256,4096]{1,0:T(8,128)(2,1)} %hidden.1.refs_4_.refs_0_.refs_2_, bf16[2,4096,1024]{2,1,0:T(8,128)(2,1)S(1)} %masked_pair.1.refs_1_.refs_3_, bf16[256,4096]{1,0:T(8,128)(2,1)} %collective-permute-done.1.refs_2_.refs_4_), custom_call_target="tpu_custom_call" | custom-call | flops 1 | bytes 1 | tf_op jit(solution)/shard_map/forward_own/pallas_call | solution.py:84
  36.1 6.2 %copy-done = bf16[2,4096,1024]{2,1,0:T(8,128)(2,1)} copy-done((bf16[2,4096,1024]{2,1,0:T(8,128)(2,1)}, bf16[2,4096,1024]{2,1,0:T(8,128)(2,1)S(1)}, u32[]{:S(2)}) %copy-start) | copy-done | bytes 16777240
  42.2 16.0 %all-gather.2.cloned.1.call-done.refs_1_ = bf16[256,4096]{1,0:T(8,128)(2,1)} async-done(((bf16[256,1024]{1,0:T(8,128)(2,1)}), bf16[256,4096]{1,0:T(8,128)(2,1)}) %all-gather.2.cloned.1.call-update) | async-done | bytes 2097168 | tf_op jit(solution)/shard_map/all_gather | solution.py:331
  58.2 2.7 %cut.1 = (bf16[256,2048]{1,0:T(8,128)(2,1)S(1)}, bf16[256,2048]{1,0:T(8,128)(2,1)}) custom-call(s32[3]{0:T(128)S(1)} %pad_add_fusion.refs_0_, bf16[256,4096]{1,0:T(8,128)(2,1)} %all-gather.2.cloned.1.call-done.refs_1_, bf16[2,256,1024]{2,1,0:T(8,128)(2,1)S(1)} %forward_own.1.refs_2_.refs_1_), custom_call_target="tpu_custom_call" | custom-call | flops 1 | bytes 1 | tf_op jit(solution)/shard_map/cut/pallas_call | solution.py:84
  61.0 1.5 collective-permute-start.4
  62.5 5.8 %copy-done.1 = bf16[2,4096,1024]{2,1,0:T(8,128)(2,1)S(1)} copy-done((bf16[2,4096,1024]{2,1,0:T(8,128)(2,1)S(1)}, bf16[2,4096,1024]{2,1,0:T(8,128)(2,1)}, u32[]{:S(2)}) %copy-start.1) | copy-done | bytes 16777240
  68.2 7.6 %forward_both.1 = (bf16[4,256,1024]{2,1,0:T(8,128)(2,1)}, bf16[256,4096]{1,0:T(8,128)(2,1)}) custom-call(s32[3]{0:T(128)S(1)} %pad_add_fusion.refs_0_, bf16[2,256,1024]{2,1,0:T(8,128)(2,1)S(1)} %forward_own.1.refs_2_.refs_1_, bf16[256,4096]{1,0:T(8,128)(2,1)} %collective-permute-done.2.refs_2_, ...), custom_call_target="tpu_custom_call", output_to_operand_aliasing={{1}: (2, {})} | custom-call | flops 1 | bytes 1 | tf_op jit(solution)/shard_map/forward_both/pallas_call | solution.py:84
  75.8 0.6 per_core.2
  76.5 5.8 %copy-done.2 = bf16[2,4096,1024]{2,1,0:T(8,128)(2,1)S(1)} copy-done((bf16[2,4096,1024]{2,1,0:T(8,128)(2,1)S(1)}, bf16[2,4096,1024]{2,1,0:T(8,128)(2,1)}, u32[]{:S(2)}) %copy-start.2) | copy-done | bytes 16777240
  82.3 4.4 %back.5.refs_2_.refs_0_ = f32[256,2560]{1,0:T(8,128)} custom-call(bf16[256,2048]{1,0:T(8,128)(2,1)S(1)} %get-tuple-element.18.refs_4_.refs_1_.refs_0_, bf16[2,4096,1024]{2,1,0:T(8,128)(2,1)S(1)} %copy-done.2, bf16[256,1024]{1,0:T(8,128)(2,1)S(1)} %get-tuple-element.21.refs_2_.refs_6_), custom_call_target="tpu_custom_call" | custom-call | flops 1 | bytes 1 | tf_op jit(solution)/shard_map/back/pallas_call | solution.py:84
  86.7 4.0 %back.6.refs_2_ = bf16[256,2560]{1,0:T(8,128)(2,1)} custom-call(bf16[256,2048]{1,0:T(8,128)(2,1)S(1)} %collective-permute-done.4.refs_0_.refs_1_, bf16[2,4096,1024]{2,1,0:T(8,128)(2,1)S(1)} %copy-done.2, f32[256,2560]{1,0:T(8,128)} %back.5.refs_2_.refs_0_), custom_call_target="tpu_custom_call" | custom-call | flops 199999995904 | bytes 1 | tf_op jit(solution)/shard_map/back/pallas_call | solution.py:84
  90.6 1.5 collective-permute-start.10
  92.1 1.5 back.7.refs_2_
  93.6 0.7 back.8.refs_2_
  96.2 0.9 slice-done.2
  97.1 1.2 slice-done.3
  98.3 3.0 %back.9.refs_10_.refs_0_ = f32[256,1536]{1,0:T(8,128)} custom-call(bf16[256,2048]{1,0:T(8,128)(2,1)S(1)} %get-tuple-element.18.refs_4_.refs_1_.refs_0_, bf16[2,4096,1024]{2,1,0:T(8,128)(2,1)S(1)} %bitcast.5, bf16[256,1024]{1,0:T(8,128)(2,1)S(1)} %get-tuple-element.23.refs_2_.refs_7_), custom_call_target="tpu_custom_call" | custom-call | flops 1 | bytes 1 | tf_op jit(solution)/shard_map/back/pallas_call | solution.py:84
  101.3 15.2 %weight_grad.1.refs_1_.refs_4_ = f32[4096,1024]{1,0:T(8,128)} custom-call(s32[3]{0:T(128)S(1)} %pad_add_fusion.refs_0_, s32[32,32]{1,0:T(8,128)S(1)} %copy-done.5, bf16[256,4096]{1,0:T(8,128)(2,1)} %hidden.1.refs_4_.refs_0_.refs_2_, bf16[256,4096]{1,0:T(8,128)(2,1)} %get-tuple-element.20.refs_3_, bf16[256,4096]{1,0:T(8,128)(2,1)} %collective-permute-done.1.refs_2_.refs_4_, ...), custom_call_target="tpu_custom_call" | custom-call | flops 1 | bytes 1 | tf_op jit(solution)/shard_map/weight_grad/pallas_call | solution.py:84
  116.5 4.9 %reduce-scatter.2.cloned.1.call-done = bf16[1,256,1024]{2,1,0:T(8,128)(2,1)} async-done(((bf16[4,256,1024]{2,1,0:T(8,128)(2,1)}), bf16[1,256,1024]{2,1,0:T(8,128)(2,1)}) %reduce-scatter.2.cloned.1.call-update) | async-done | bytes 524304 | tf_op jit(solution)/shard_map/reduce_scatter | solution.py:340
  121.4 1.0 copy-done.3
  122.5 0.7 collective-permute-start.7
  123.2 4.2 %collective-permute-start.8 = (bf16[256,512]{1,0:T(8,128)(2,1)S(1)}, bf16[256,512]{1,0:T(8,128)(2,1)S(1)}, u32[]{:S(2)}, u32[]{:S(2)}) collective-permute-start(bf16[256,512]{1,0:T(8,128)(2,1)S(1)} %back.8.refs_2_), channel_id=1, source_target_pairs={{0,8},{4,12},{8,0},{12,4},{1,9},{5,13},{9,1},{13,5},{2,10},{6,14},... | collective-permute-start | bytes 786440 | tf_op jit(solution)/shard_map/ppermute | solution.py:316
  127.5 6.1 %hidden_grads.3 = (bf16[256,4096]{1,0:T(8,128)(2,1)}, bf16[256,4096]{1,0:T(8,128)(2,1)}) custom-call(f32[256,2560]{1,0:T(8,128)} %back.5.refs_2_.refs_0_, bf16[256,2560]{1,0:T(8,128)(2,1)} %collective-permute-done.10.refs_1_, bf16[256,4096]{1,0:T(8,128)(2,1)} %refs_2_.7, bf16[256,4096]{1,0:T(8,128)(2,1)} %refs_3_.5, f32[4096,1024]{1,0:T(8,128)} %weight_grad.1.refs_1_.refs_4_), custom_call_target="tpu_custom_call" | custom-call | flops 1 | bytes 1 | tf_op jit(solution)/shard_map/hidden_grads/pallas_call | solution.py:84
  133.6 10.3 %collective-permute-done.9.refs_1_ = bf16[256,1024]{1,0:T(8,128)(2,1)S(1)} collective-permute-done((bf16[256,1024]{1,0:T(8,128)(2,1)S(1)}, bf16[256,1024]{1,0:T(8,128)(2,1)S(1)}, u32[]{:S(2)}, u32[]{:S(2)}) %collective-permute-start.9) | collective-permute-done | bytes 524320 | tf_op jit(solution)/shard_map/ppermute | solution.py:316
  143.9 2.5 %hidden_grads.4 = (bf16[256,4096]{1,0:T(8,128)(2,1)}, bf16[256,4096]{1,0:T(8,128)(2,1)}) custom-call(f32[256,1536]{1,0:T(8,128)} %back.9.refs_10_.refs_0_, bf16[256,1024]{1,0:T(8,128)(2,1)S(1)} %collective-permute-done.9.refs_1_, bf16[256,4096]{1,0:T(8,128)(2,1)} %refs_2_.7, ...), custom_call_target="tpu_custom_call", output_to_operand_aliasing={{0}: (4, {}), {1}: (5, {})} | custom-call | flops 1 | bytes 1 | tf_op jit(solution)/shard_map/hidden_grads/pallas_call | solution.py:84
  146.4 2.7 %collective-permute-done.8.refs_1_ = bf16[256,512]{1,0:T(8,128)(2,1)S(1)} collective-permute-done((bf16[256,512]{1,0:T(8,128)(2,1)S(1)}, bf16[256,512]{1,0:T(8,128)(2,1)S(1)}, u32[]{:S(2)}, u32[]{:S(2)}) %collective-permute-start.8) | collective-permute-done | bytes 262176 | tf_op jit(solution)/shard_map/ppermute | solution.py:316
  149.1 2.2 %hidden_grads.5 = (bf16[256,4096]{1,0:T(8,128)(2,1)}, bf16[256,4096]{1,0:T(8,128)(2,1)}) custom-call(f32[256,1536]{1,0:T(8,128)} %back.9.refs_10_.refs_0_, bf16[256,512]{1,0:T(8,128)(2,1)S(1)} %collective-permute-done.8.refs_1_, bf16[256,4096]{1,0:T(8,128)(2,1)} %refs_2_.7, bf16[256,4096]{1,0:T(8,128)(2,1)} %refs_3_.5, ...), custom_call_target="tpu_custom_call", output_to_operand_aliasing={{0}: (4, {}), {1}: (5, {})} | custom-call | flops 1 | bytes 1 | tf_op jit(solution)/shard_map/hidden_grads/pallas_call | solution.py:84
  151.3 1.4 choose.1
  (36 shorter events, 3.3 us)
Async XLA Ops:
  7.2 51.1 %all-gather.2.cloned.1.call-start = ((), (), s32[]{:S(2)}) async-start(), calls=%async_computation.1 | async-start | bytes 2621440 | tf_op jit(solution)/shard_map/all_gather | solution.py:331
  7.2 13.6 %collective-permute-start = (bf16[4096,1024]{1,0:T(8,128)(2,1)}, bf16[4096,1024]{1,0:T(8,128)(2,1)}, u32[]{:S(2)}, u32[]{:S(2)}) collective-permute-start(bf16[4096,1024]{1,0:T(8,128)(2,1)} %refs_2_.4), channel_id=1, source_target_pairs={{0,4},{4,0},{8,12},{12,8},{1,5},{5,1},{9,13},{13,9},{2,6},{6,2},{1... | collective-permute-start | bytes 25165832 | tf_op jit(solution)/shard_map/ppermute | solution.py:319
  7.9 13.0 %copy-start.4 = (s32[32,32]{1,0:T(8,128)S(1)}, s32[32,32]{1,0:T(8,128)}, u32[]{:S(2)}) copy-start(s32[32,32]{1,0:T(8,128)} %refs_1_.5) | copy-start | bytes 12292
  7.9 113.5 %reduce-scatter.2.cloned.1.call-start = ((), (), s32[]{:S(2)}) async-start(), calls=%async_computation.2 | async-start | bytes 2621440 | tf_op jit(solution)/shard_map/reduce_scatter | solution.py:340
  12.6 17.2 %collective-permute-start.1 = (bf16[256,4096]{1,0:T(8,128)(2,1)}, bf16[256,4096]{1,0:T(8,128)(2,1)}, u32[]{:S(2)}, u32[]{:S(2)}) collective-permute-start(bf16[256,4096]{1,0:T(8,128)(2,1)} %hidden.1.refs_4_.refs_0_.refs_2_), channel_id=1, source_target_pairs={{0,4},{4,0},{8,12},{12,8},{1,5},{5,1},{9,13},{13,9},{2,6},{6,2},{1... | collective-permute-start | bytes 6291464 | tf_op jit(solution)/shard_map/ppermute | solution.py:319
  13.1 49.4 %collective-permute-start.2 = (bf16[256,4096]{1,0:T(8,128)(2,1)}, bf16[256,4096]{1,0:T(8,128)(2,1)}, u32[]{:S(2)}, u32[]{:S(2)}) collective-permute-start(bf16[256,4096]{1,0:T(8,128)(2,1)} %hidden.1.refs_4_.refs_0_.refs_2_), channel_id=1, source_target_pairs={{0,8},{4,12},{8,0},{12,4},{1,9},{5,13},{9,1},{13,5},{2,10},{6,14},... | collective-permute-start | bytes 6291464 | tf_op jit(solution)/shard_map/ppermute | solution.py:316
  36.0 6.2 %copy-start = (bf16[2,4096,1024]{2,1,0:T(8,128)(2,1)}, bf16[2,4096,1024]{2,1,0:T(8,128)(2,1)S(1)}, u32[]{:S(2)}) copy-start(bf16[2,4096,1024]{2,1,0:T(8,128)(2,1)S(1)} %masked_pair.1.refs_1_.refs_3_) | copy-start | bytes 50331652
  61.0 25.7 %collective-permute-start.4 = (bf16[256,2048]{1,0:T(8,128)(2,1)}, bf16[256,2048]{1,0:T(8,128)(2,1)S(1)}, u32[]{:S(2)}, u32[]{:S(2)}) collective-permute-start(bf16[256,2048]{1,0:T(8,128)(2,1)} %get-tuple-element.22), channel_id=1, source_target_pairs={{0,8},{4,12},{8,0},{12,4},{1,9},{5,13},{9,1},{13,5},{2,10},{6,14},... | collective-permute-start | bytes 3145736 | tf_op jit(solution)/shard_map/ppermute | solution.py:316
  62.5 5.8 %copy-start.1 = (bf16[2,4096,1024]{2,1,0:T(8,128)(2,1)S(1)}, bf16[2,4096,1024]{2,1,0:T(8,128)(2,1)}, u32[]{:S(2)}) copy-start(bf16[2,4096,1024]{2,1,0:T(8,128)(2,1)} %copy-done) | copy-start | bytes 50331652
  76.4 24.8 %collective-permute-start.3 = (bf16[256,4096]{1,0:T(8,128)(2,1)}, bf16[256,4096]{1,0:T(8,128)(2,1)}, u32[]{:S(2)}, u32[]{:S(2)}) collective-permute-start(bf16[256,4096]{1,0:T(8,128)(2,1)} %get-tuple-element.20.refs_3_), channel_id=1, source_target_pairs={{0,4},{4,0},{8,12},{12,8},{1,5},{5,1},{9,13},{13,9},{2,6},{6,2},{1... | collective-permute-start | bytes 6291464 | tf_op jit(solution)/shard_map/ppermute | solution.py:319
  76.5 5.8 %copy-start.2 = (bf16[2,4096,1024]{2,1,0:T(8,128)(2,1)S(1)}, bf16[2,4096,1024]{2,1,0:T(8,128)(2,1)}, u32[]{:S(2)}) copy-start(bf16[2,4096,1024]{2,1,0:T(8,128)(2,1)} %copy-done) | copy-start | bytes 50331652
  90.6 36.8 %collective-permute-start.10 = (bf16[256,2560]{1,0:T(8,128)(2,1)}, bf16[256,2560]{1,0:T(8,128)(2,1)}, u32[]{:S(2)}, u32[]{:S(2)}) collective-permute-start(bf16[256,2560]{1,0:T(8,128)(2,1)} %back.6.refs_2_), channel_id=1, source_target_pairs={{0,8},{4,12},{8,0},{12,4},{1,9},{5,13},{9,1},{13,5},{2,10},{6,14},... | collective-permute-start | bytes 3932168 | tf_op jit(solution)/shard_map/ppermute | solution.py:316
  92.1 4.1 %slice-start = ((s8[16777216]{0:T(1024)(128)(4,1)}), s8[4194304]{0:T(1024)(128)(4,1)S(1)}, s32[]{:S(2)}) async-start(s8[16777216]{0:T(1024)(128)(4,1)} %bitcast.4), calls=%async_computation.3 | async-start | bytes 8388608
  92.1 4.1 %slice-start.1 = ((s8[16777216]{0:T(1024)(128)(4,1)}), s8[4194304]{0:T(1024)(128)(4,1)S(1)}, s32[]{:S(2)}) async-start(s8[16777216]{0:T(1024)(128)(4,1)} %bitcast.4), calls=%async_computation.4 | async-start | bytes 8388608
  93.6 3.5 %slice-start.2 = ((s8[16777216]{0:T(1024)(128)(4,1)}), s8[4194304]{0:T(1024)(128)(4,1)S(1)}, s32[]{:S(2)}) async-start(s8[16777216]{0:T(1024)(128)(4,1)} %bitcast.4), calls=%async_computation.5 | async-start | bytes 8388608
  93.6 4.7 %slice-start.3 = ((s8[16777216]{0:T(1024)(128)(4,1)}), s8[4194304]{0:T(1024)(128)(4,1)S(1)}, s32[]{:S(2)}) async-start(s8[16777216]{0:T(1024)(128)(4,1)} %bitcast.4), calls=%async_computation.6 | async-start | bytes 8388608
  94.3 6.9 %collective-permute-start.5 = (bf16[256,1024]{1,0:T(8,128)(2,1)S(1)}, bf16[256,1024]{1,0:T(8,128)(2,1)S(1)}, u32[]{:S(2)}, u32[]{:S(2)}) collective-permute-start(bf16[256,1024]{1,0:T(8,128)(2,1)S(1)} %get-tuple-element.24), channel_id=1, source_target_pairs={{0,4},{4,0},{8,12},{12,8},{1,5},{5,1},{9,13},{13,9},{2,6},{6,2},{1... | collective-permute-start | bytes 1572872 | tf_op jit(solution)/shard_map/ppermute | solution.py:319
  95.2 6.0 %collective-permute-start.6 = (bf16[256,1024]{1,0:T(8,128)(2,1)S(1)}, bf16[256,1024]{1,0:T(8,128)(2,1)S(1)}, u32[]{:S(2)}, u32[]{:S(2)}) collective-permute-start(bf16[256,1024]{1,0:T(8,128)(2,1)S(1)} %get-tuple-element.25), channel_id=1, source_target_pairs={{0,4},{4,0},{8,12},{12,8},{1,5},{5,1},{9,13},{13,9},{2,6},{6,2},{1... | collective-permute-start | bytes 1572872 | tf_op jit(solution)/shard_map/ppermute | solution.py:319
  95.6 48.3 %collective-permute-start.9 = (bf16[256,1024]{1,0:T(8,128)(2,1)S(1)}, bf16[256,1024]{1,0:T(8,128)(2,1)S(1)}, u32[]{:S(2)}, u32[]{:S(2)}) collective-permute-start(bf16[256,1024]{1,0:T(8,128)(2,1)S(1)} %back.7.refs_2_), channel_id=1, source_target_pairs={{0,8},{4,12},{8,0},{12,4},{1,9},{5,13},{9,1},{13,5},{2,10},{6,14},... | collective-permute-start | bytes 1572872 | tf_op jit(solution)/shard_map/ppermute | solution.py:316
  98.3 3.0 %copy-start.5 = (s32[32,32]{1,0:T(8,128)S(1)}, s32[32,32]{1,0:T(8,128)}, u32[]{:S(2)}) copy-start(s32[32,32]{1,0:T(8,128)} %refs_1_.5) | copy-start | bytes 12292
  121.4 1.0 copy-start.3
  122.5 28.8 %collective-permute-start.7 = (bf16[256,1024]{1,0:T(8,128)(2,1)S(1)}, bf16[256,1024]{1,0:T(8,128)(2,1)S(1)}, u32[]{:S(2)}, u32[]{:S(2)}) collective-permute-start(bf16[256,1024]{1,0:T(8,128)(2,1)S(1)} %relay.1.refs_1_), channel_id=1, source_target_pairs={{1,9},{2,1},{3,8},{5,13},{6,5},{7,12},{10,2},{9,10},{8,3},{14,6},{... | collective-permute-start | bytes 1572872 | tf_op jit(solution)/shard_map/ppermute | solution.py:328
  123.2 25.9 %collective-permute-start.8 = (bf16[256,512]{1,0:T(8,128)(2,1)S(1)}, bf16[256,512]{1,0:T(8,128)(2,1)S(1)}, u32[]{:S(2)}, u32[]{:S(2)}) collective-permute-start(bf16[256,512]{1,0:T(8,128)(2,1)S(1)} %back.8.refs_2_), channel_id=1, source_target_pairs={{0,8},{4,12},{8,0},{12,4},{1,9},{5,13},{9,1},{13,5},{2,10},{6,14},... | collective-permute-start | bytes 786440 | tf_op jit(solution)/shard_map/ppermute | solution.py:316
Sparse Core Ops, SparseCore 0:
  9.6 48.6 all-gather.1
  75.9 45.4 reduce-scatter.1

commit v4 on v3

--- a/solution.py
+++ b/solution.py
@@ -108,7 +108,7 @@
 
 def hidden_of(gate, up, deps):
     rows, hid = gate.shape
-    unit = 64
+    unit = 128
 
     def body(gate_ref, up_ref, out):
         g = gate_ref[...].astype(F32)

time: 160 us -> 159 us (level)
  transfers between devices with their start and end apart: 13 -> 13, of which waited for: 5 -> 5; matrix products, arithmetic and copies ran while one was open for 0% -> 0% of each run, Pallas kernels for 45% -> 44%
where the time goes in v4:
time: 159 us
  Pallas kernels  71.3 us (45%)
  waiting for transfers between devices  40.2 us (25%)
  local copies, waits for them, and re-layouts  20.2 us (13%)
  between operations  14.2 us (9%)
  starting transfers between devices  12.7 us (8%)
    pallas_call x18, Pallas kernels, ordered(): pl.pallas_call(run, grid=grid, in_specs=in_specs + [ANYWHERE] * m, out_sp...  71.3 us
    unnamed x20, local copies, waits for them, and re-layouts  20.2 us
    all_gather x1, waiting for transfers between devices, four_by_four(): full_grad = lax.all_gather(grad_out, 'tensor', axis=1, tiled=True)  16 us
    ppermute x5, waiting for transfers between devices, over_x(): return lax.ppermute(a, 'dp', [(i, i ^ 2) for i in range(4)])  13.5 us
    ppermute x5, starting transfers between devices, over_x(): return lax.ppermute(a, 'dp', [(i, i ^ 2) for i in range(4)])  10.2 us
    ppermute x5, waiting for transfers between devices, over_core(): return lax.ppermute(a, 'dp', [(i, i ^ 1) for i in range(4)])  6.28 us
    reduce_scatter x1, waiting for transfers between devices, four_by_four(): out = lax.psum_scatter(o_all, 'tensor', scatter_dimension=0, tiled=False)  4.17 us
  transfers between devices with their start and end apart: 13, of which 5 were waited for; matrix products, arithmetic and copies ran while one was open for 0% of the time, Pallas kernels for 44%

profile of v4, /device:TPU:0, one launch (start us, length us, event | category | flops | bytes accessed | tf_op | source)
XLA Modules:
  0.0 158.6 jit_solution(7327922649754284427)
XLA Ops:
  8.0 3.6 %hidden.1.refs_4_.refs_0_.refs_2_ = bf16[256,4096]{1,0:T(8,128)(2,1)} custom-call(bf16[256,4096]{1,0:T(8,128)(2,1)} %refs_2_.7, bf16[256,4096]{1,0:T(8,128)(2,1)} %refs_3_.5), custom_call_target="tpu_custom_call" | custom-call | flops 1 | bytes 1 | tf_op jit(solution)/shard_map/hidden/pallas_call | solution.py:84
  12.0 2.5 %collective-permute-start.2 = (bf16[256,4096]{1,0:T(8,128)(2,1)}, bf16[256,4096]{1,0:T(8,128)(2,1)}, u32[]{:S(2)}, u32[]{:S(2)}) collective-permute-start(bf16[256,4096]{1,0:T(8,128)(2,1)} %hidden.1.refs_4_.refs_0_.refs_2_), channel_id=1, source_target_pairs={{0,8},{4,12},{8,0},{12,4},{1,9},{5,13},{9,1},{13,5},{2,10},{6,14},... | collective-permute-start | bytes 6291464 | tf_op jit(solution)/shard_map/ppermute | solution.py:316
  14.6 6.3 %collective-permute-done.refs_3_ = bf16[4096,1024]{1,0:T(8,128)(2,1)} collective-permute-done((bf16[4096,1024]{1,0:T(8,128)(2,1)}, bf16[4096,1024]{1,0:T(8,128)(2,1)}, u32[]{:S(2)}, u32[]{:S(2)}) %collective-permute-start) | collective-permute-done | bytes 8388640 | tf_op jit(solution)/shard_map/ppermute | solution.py:319
  20.9 9.0 %masked_pair.1.refs_1_.refs_3_ = bf16[2,4096,1024]{2,1,0:T(8,128)(2,1)S(1)} custom-call(s32[3]{0:T(128)S(1)} %pad_add_fusion.refs_0_, s32[32,32]{1,0:T(8,128)S(1)} %copy-done.4, bf16[4096,1024]{1,0:T(8,128)(2,1)} %refs_2_.4, bf16[4096,1024]{1,0:T(8,128)(2,1)} %collective-permute-done.refs_3_, bf16[256,4096]{1,0:T(8,128)(2,1)} %hidden.1.refs_4_.refs_0_.refs_2_), custom_call_target="tpu_custom_call" | custom-call | flops 1 | bytes 1 | tf_op jit(solution)/shard_map/masked_pair/pallas_call | solution.py:84
  29.8 6.2 %forward_own.1.refs_2_.refs_1_ = bf16[2,256,1024]{2,1,0:T(8,128)(2,1)S(1)} custom-call(bf16[256,4096]{1,0:T(8,128)(2,1)} %hidden.1.refs_4_.refs_0_.refs_2_, bf16[2,4096,1024]{2,1,0:T(8,128)(2,1)S(1)} %masked_pair.1.refs_1_.refs_3_, bf16[256,4096]{1,0:T(8,128)(2,1)} %collective-permute-done.1.refs_2_.refs_4_), custom_call_target="tpu_custom_call" | custom-call | flops 1 | bytes 1 | tf_op jit(solution)/shard_map/forward_own/pallas_call | solution.py:84
  36.1 6.2 %copy-done = bf16[2,4096,1024]{2,1,0:T(8,128)(2,1)} copy-done((bf16[2,4096,1024]{2,1,0:T(8,128)(2,1)}, bf16[2,4096,1024]{2,1,0:T(8,128)(2,1)S(1)}, u32[]{:S(2)}) %copy-start) | copy-done | bytes 16777240
  42.2 16.0 %all-gather.2.cloned.1.call-done.refs_1_ = bf16[256,4096]{1,0:T(8,128)(2,1)} async-done(((bf16[256,1024]{1,0:T(8,128)(2,1)}), bf16[256,4096]{1,0:T(8,128)(2,1)}) %all-gather.2.cloned.1.call-update) | async-done | bytes 2097168 | tf_op jit(solution)/shard_map/all_gather | solution.py:331
  58.2 2.7 %cut.1 = (bf16[256,2048]{1,0:T(8,128)(2,1)S(1)}, bf16[256,2048]{1,0:T(8,128)(2,1)}) custom-call(s32[3]{0:T(128)S(1)} %pad_add_fusion.refs_0_, bf16[256,4096]{1,0:T(8,128)(2,1)} %all-gather.2.cloned.1.call-done.refs_1_, bf16[2,256,1024]{2,1,0:T(8,128)(2,1)S(1)} %forward_own.1.refs_2_.refs_1_), custom_call_target="tpu_custom_call" | custom-call | flops 1 | bytes 1 | tf_op jit(solution)/shard_map/cut/pallas_call | solution.py:84
  61.0 1.5 collective-permute-start.4
  62.5 5.8 %copy-done.1 = bf16[2,4096,1024]{2,1,0:T(8,128)(2,1)S(1)} copy-done((bf16[2,4096,1024]{2,1,0:T(8,128)(2,1)S(1)}, bf16[2,4096,1024]{2,1,0:T(8,128)(2,1)}, u32[]{:S(2)}) %copy-start.1) | copy-done | bytes 16777240
  68.2 7.6 %forward_both.1 = (bf16[4,256,1024]{2,1,0:T(8,128)(2,1)}, bf16[256,4096]{1,0:T(8,128)(2,1)}) custom-call(s32[3]{0:T(128)S(1)} %pad_add_fusion.refs_0_, bf16[2,256,1024]{2,1,0:T(8,128)(2,1)S(1)} %forward_own.1.refs_2_.refs_1_, bf16[256,4096]{1,0:T(8,128)(2,1)} %collective-permute-done.2.refs_2_, ...), custom_call_target="tpu_custom_call", output_to_operand_aliasing={{1}: (2, {})} | custom-call | flops 1 | bytes 1 | tf_op jit(solution)/shard_map/forward_both/pallas_call | solution.py:84
  75.8 0.6 per_core.2
  76.5 5.9 %copy-done.2 = bf16[2,4096,1024]{2,1,0:T(8,128)(2,1)S(1)} copy-done((bf16[2,4096,1024]{2,1,0:T(8,128)(2,1)S(1)}, bf16[2,4096,1024]{2,1,0:T(8,128)(2,1)}, u32[]{:S(2)}) %copy-start.2) | copy-done | bytes 16777240
  82.4 4.4 %back.5.refs_2_.refs_0_ = f32[256,2560]{1,0:T(8,128)} custom-call(bf16[256,2048]{1,0:T(8,128)(2,1)S(1)} %get-tuple-element.18.refs_4_.refs_1_.refs_0_, bf16[2,4096,1024]{2,1,0:T(8,128)(2,1)S(1)} %copy-done.2, bf16[256,1024]{1,0:T(8,128)(2,1)S(1)} %get-tuple-element.21.refs_2_.refs_6_), custom_call_target="tpu_custom_call" | custom-call | flops 1 | bytes 1 | tf_op jit(solution)/shard_map/back/pallas_call | solution.py:84
  86.8 4.0 %back.6.refs_2_ = bf16[256,2560]{1,0:T(8,128)(2,1)} custom-call(bf16[256,2048]{1,0:T(8,128)(2,1)S(1)} %collective-permute-done.4.refs_0_.refs_1_, bf16[2,4096,1024]{2,1,0:T(8,128)(2,1)S(1)} %copy-done.2, f32[256,2560]{1,0:T(8,128)} %back.5.refs_2_.refs_0_), custom_call_target="tpu_custom_call" | custom-call | flops 199999995904 | bytes 1 | tf_op jit(solution)/shard_map/back/pallas_call | solution.py:84
  90.7 0.7 collective-permute-start.10
  91.5 1.5 back.7.refs_2_
  93.0 0.7 back.8.refs_2_
  95.0 1.3 collective-permute-start.9
  96.4 1.2 slice-done.3
  97.6 3.0 %back.9.refs_10_.refs_0_ = f32[256,1536]{1,0:T(8,128)} custom-call(bf16[256,2048]{1,0:T(8,128)(2,1)S(1)} %get-tuple-element.18.refs_4_.refs_1_.refs_0_, bf16[2,4096,1024]{2,1,0:T(8,128)(2,1)S(1)} %bitcast.5, bf16[256,1024]{1,0:T(8,128)(2,1)S(1)} %get-tuple-element.23.refs_2_.refs_7_), custom_call_target="tpu_custom_call" | custom-call | flops 1 | bytes 1 | tf_op jit(solution)/shard_map/back/pallas_call | solution.py:84
  100.6 15.2 %weight_grad.1.refs_1_.refs_4_ = f32[4096,1024]{1,0:T(8,128)} custom-call(s32[3]{0:T(128)S(1)} %pad_add_fusion.refs_0_, s32[32,32]{1,0:T(8,128)S(1)} %copy-done.5, bf16[256,4096]{1,0:T(8,128)(2,1)} %hidden.1.refs_4_.refs_0_.refs_2_, bf16[256,4096]{1,0:T(8,128)(2,1)} %get-tuple-element.20.refs_3_, bf16[256,4096]{1,0:T(8,128)(2,1)} %collective-permute-done.1.refs_2_.refs_4_, ...), custom_call_target="tpu_custom_call" | custom-call | flops 1 | bytes 1 | tf_op jit(solution)/shard_map/weight_grad/pallas_call | solution.py:84
  115.8 4.2 %reduce-scatter.2.cloned.1.call-done = bf16[1,256,1024]{2,1,0:T(8,128)(2,1)} async-done(((bf16[4,256,1024]{2,1,0:T(8,128)(2,1)}), bf16[1,256,1024]{2,1,0:T(8,128)(2,1)}) %reduce-scatter.2.cloned.1.call-update) | async-done | bytes 524304 | tf_op jit(solution)/shard_map/reduce_scatter | solution.py:340
  120.0 1.0 copy-done.3
  121.1 0.7 collective-permute-start.7
  121.8 4.3 %collective-permute-start.8 = (bf16[256,512]{1,0:T(8,128)(2,1)S(1)}, bf16[256,512]{1,0:T(8,128)(2,1)S(1)}, u32[]{:S(2)}, u32[]{:S(2)}) collective-permute-start(bf16[256,512]{1,0:T(8,128)(2,1)S(1)} %back.8.refs_2_), channel_id=1, source_target_pairs={{0,8},{4,12},{8,0},{12,4},{1,9},{5,13},{9,1},{13,5},{2,10},{6,14},... | collective-permute-start | bytes 786440 | tf_op jit(solution)/shard_map/ppermute | solution.py:316
  126.0 6.1 %hidden_grads.3 = (bf16[256,4096]{1,0:T(8,128)(2,1)}, bf16[256,4096]{1,0:T(8,128)(2,1)}) custom-call(f32[256,2560]{1,0:T(8,128)} %back.5.refs_2_.refs_0_, bf16[256,2560]{1,0:T(8,128)(2,1)} %collective-permute-done.10.refs_1_, bf16[256,4096]{1,0:T(8,128)(2,1)} %refs_2_.7, bf16[256,4096]{1,0:T(8,128)(2,1)} %refs_3_.5, f32[4096,1024]{1,0:T(8,128)} %weight_grad.1.refs_1_.refs_4_), custom_call_target="tpu_custom_call" | custom-call | flops 1 | bytes 1 | tf_op jit(solution)/shard_map/hidden_grads/pallas_call | solution.py:84
  132.1 11.1 %collective-permute-done.9.refs_1_ = bf16[256,1024]{1,0:T(8,128)(2,1)S(1)} collective-permute-done((bf16[256,1024]{1,0:T(8,128)(2,1)S(1)}, bf16[256,1024]{1,0:T(8,128)(2,1)S(1)}, u32[]{:S(2)}, u32[]{:S(2)}) %collective-permute-start.9) | collective-permute-done | bytes 524320 | tf_op jit(solution)/shard_map/ppermute | solution.py:316
  143.3 2.5 %hidden_grads.4 = (bf16[256,4096]{1,0:T(8,128)(2,1)}, bf16[256,4096]{1,0:T(8,128)(2,1)}) custom-call(f32[256,1536]{1,0:T(8,128)} %back.9.refs_10_.refs_0_, bf16[256,1024]{1,0:T(8,128)(2,1)S(1)} %collective-permute-done.9.refs_1_, bf16[256,4096]{1,0:T(8,128)(2,1)} %refs_2_.7, ...), custom_call_target="tpu_custom_call", output_to_operand_aliasing={{0}: (4, {}), {1}: (5, {})} | custom-call | flops 1 | bytes 1 | tf_op jit(solution)/shard_map/hidden_grads/pallas_call | solution.py:84
  145.8 2.3 %collective-permute-done.8.refs_1_ = bf16[256,512]{1,0:T(8,128)(2,1)S(1)} collective-permute-done((bf16[256,512]{1,0:T(8,128)(2,1)S(1)}, bf16[256,512]{1,0:T(8,128)(2,1)S(1)}, u32[]{:S(2)}, u32[]{:S(2)}) %collective-permute-start.8) | collective-permute-done | bytes 262176 | tf_op jit(solution)/shard_map/ppermute | solution.py:316
  148.2 2.2 %hidden_grads.5 = (bf16[256,4096]{1,0:T(8,128)(2,1)}, bf16[256,4096]{1,0:T(8,128)(2,1)}) custom-call(f32[256,1536]{1,0:T(8,128)} %back.9.refs_10_.refs_0_, bf16[256,512]{1,0:T(8,128)(2,1)S(1)} %collective-permute-done.8.refs_1_, bf16[256,4096]{1,0:T(8,128)(2,1)} %refs_2_.7, bf16[256,4096]{1,0:T(8,128)(2,1)} %refs_3_.5, ...), custom_call_target="tpu_custom_call", output_to_operand_aliasing={{0}: (4, {}), {1}: (5, {})} | custom-call | flops 1 | bytes 1 | tf_op jit(solution)/shard_map/hidden_grads/pallas_call | solution.py:84
  150.4 1.4 choose.1
  (36 shorter events, 2.8 us)
Async XLA Ops:
  7.2 51.1 %all-gather.2.cloned.1.call-start = ((), (), s32[]{:S(2)}) async-start(), calls=%async_computation.1 | async-start | bytes 2621440 | tf_op jit(solution)/shard_map/all_gather | solution.py:331
  7.2 13.6 %collective-permute-start = (bf16[4096,1024]{1,0:T(8,128)(2,1)}, bf16[4096,1024]{1,0:T(8,128)(2,1)}, u32[]{:S(2)}, u32[]{:S(2)}) collective-permute-start(bf16[4096,1024]{1,0:T(8,128)(2,1)} %refs_2_.4), channel_id=1, source_target_pairs={{0,4},{4,0},{8,12},{12,8},{1,5},{5,1},{9,13},{13,9},{2,6},{6,2},{1... | collective-permute-start | bytes 25165832 | tf_op jit(solution)/shard_map/ppermute | solution.py:319
  7.9 13.0 %copy-start.4 = (s32[32,32]{1,0:T(8,128)S(1)}, s32[32,32]{1,0:T(8,128)}, u32[]{:S(2)}) copy-start(s32[32,32]{1,0:T(8,128)} %refs_1_.5) | copy-start | bytes 12292
  7.9 112.1 %reduce-scatter.2.cloned.1.call-start = ((), (), s32[]{:S(2)}) async-start(), calls=%async_computation.2 | async-start | bytes 2621440 | tf_op jit(solution)/shard_map/reduce_scatter | solution.py:340
  11.6 18.3 %collective-permute-start.1 = (bf16[256,4096]{1,0:T(8,128)(2,1)}, bf16[256,4096]{1,0:T(8,128)(2,1)}, u32[]{:S(2)}, u32[]{:S(2)}) collective-permute-start(bf16[256,4096]{1,0:T(8,128)(2,1)} %hidden.1.refs_4_.refs_0_.refs_2_), channel_id=1, source_target_pairs={{0,4},{4,0},{8,12},{12,8},{1,5},{5,1},{9,13},{13,9},{2,6},{6,2},{1... | collective-permute-start | bytes 6291464 | tf_op jit(solution)/shard_map/ppermute | solution.py:319
  12.0 50.4 %collective-permute-start.2 = (bf16[256,4096]{1,0:T(8,128)(2,1)}, bf16[256,4096]{1,0:T(8,128)(2,1)}, u32[]{:S(2)}, u32[]{:S(2)}) collective-permute-start(bf16[256,4096]{1,0:T(8,128)(2,1)} %hidden.1.refs_4_.refs_0_.refs_2_), channel_id=1, source_target_pairs={{0,8},{4,12},{8,0},{12,4},{1,9},{5,13},{9,1},{13,5},{2,10},{6,14},... | collective-permute-start | bytes 6291464 | tf_op jit(solution)/shard_map/ppermute | solution.py:316
  36.0 6.2 %copy-start = (bf16[2,4096,1024]{2,1,0:T(8,128)(2,1)}, bf16[2,4096,1024]{2,1,0:T(8,128)(2,1)S(1)}, u32[]{:S(2)}) copy-start(bf16[2,4096,1024]{2,1,0:T(8,128)(2,1)S(1)} %masked_pair.1.refs_1_.refs_3_) | copy-start | bytes 50331652
  61.0 25.8 %collective-permute-start.4 = (bf16[256,2048]{1,0:T(8,128)(2,1)}, bf16[256,2048]{1,0:T(8,128)(2,1)S(1)}, u32[]{:S(2)}, u32[]{:S(2)}) collective-permute-start(bf16[256,2048]{1,0:T(8,128)(2,1)} %get-tuple-element.22), channel_id=1, source_target_pairs={{0,8},{4,12},{8,0},{12,4},{1,9},{5,13},{9,1},{13,5},{2,10},{6,14},... | collective-permute-start | bytes 3145736 | tf_op jit(solution)/shard_map/ppermute | solution.py:316
  62.5 5.8 %copy-start.1 = (bf16[2,4096,1024]{2,1,0:T(8,128)(2,1)S(1)}, bf16[2,4096,1024]{2,1,0:T(8,128)(2,1)}, u32[]{:S(2)}) copy-start(bf16[2,4096,1024]{2,1,0:T(8,128)(2,1)} %copy-done) | copy-start | bytes 50331652
  76.4 24.2 %collective-permute-start.3 = (bf16[256,4096]{1,0:T(8,128)(2,1)}, bf16[256,4096]{1,0:T(8,128)(2,1)}, u32[]{:S(2)}, u32[]{:S(2)}) collective-permute-start(bf16[256,4096]{1,0:T(8,128)(2,1)} %get-tuple-element.20.refs_3_), channel_id=1, source_target_pairs={{0,4},{4,0},{8,12},{12,8},{1,5},{5,1},{9,13},{13,9},{2,6},{6,2},{1... | collective-permute-start | bytes 6291464 | tf_op jit(solution)/shard_map/ppermute | solution.py:319
  76.5 5.9 %copy-start.2 = (bf16[2,4096,1024]{2,1,0:T(8,128)(2,1)S(1)}, bf16[2,4096,1024]{2,1,0:T(8,128)(2,1)}, u32[]{:S(2)}) copy-start(bf16[2,4096,1024]{2,1,0:T(8,128)(2,1)} %copy-done) | copy-start | bytes 50331652
  90.7 35.3 %collective-permute-start.10 = (bf16[256,2560]{1,0:T(8,128)(2,1)}, bf16[256,2560]{1,0:T(8,128)(2,1)}, u32[]{:S(2)}, u32[]{:S(2)}) collective-permute-start(bf16[256,2560]{1,0:T(8,128)(2,1)} %back.6.refs_2_), channel_id=1, source_target_pairs={{0,8},{4,12},{8,0},{12,4},{1,9},{5,13},{9,1},{13,5},{2,10},{6,14},... | collective-permute-start | bytes 3932168 | tf_op jit(solution)/shard_map/ppermute | solution.py:316
  91.5 4.8 %slice-start = ((s8[16777216]{0:T(1024)(128)(4,1)}), s8[4194304]{0:T(1024)(128)(4,1)S(1)}, s32[]{:S(2)}) async-start(s8[16777216]{0:T(1024)(128)(4,1)} %bitcast.4), calls=%async_computation.3 | async-start | bytes 8388608
  91.5 4.8 %slice-start.1 = ((s8[16777216]{0:T(1024)(128)(4,1)}), s8[4194304]{0:T(1024)(128)(4,1)S(1)}, s32[]{:S(2)}) async-start(s8[16777216]{0:T(1024)(128)(4,1)} %bitcast.4), calls=%async_computation.4 | async-start | bytes 8388608
  93.0 3.5 %slice-start.2 = ((s8[16777216]{0:T(1024)(128)(4,1)}), s8[4194304]{0:T(1024)(128)(4,1)S(1)}, s32[]{:S(2)}) async-start(s8[16777216]{0:T(1024)(128)(4,1)} %bitcast.4), calls=%async_computation.5 | async-start | bytes 8388608
  93.0 4.6 %slice-start.3 = ((s8[16777216]{0:T(1024)(128)(4,1)}), s8[4194304]{0:T(1024)(128)(4,1)S(1)}, s32[]{:S(2)}) async-start(s8[16777216]{0:T(1024)(128)(4,1)} %bitcast.4), calls=%async_computation.6 | async-start | bytes 8388608
  93.7 6.9 %collective-permute-start.5 = (bf16[256,1024]{1,0:T(8,128)(2,1)S(1)}, bf16[256,1024]{1,0:T(8,128)(2,1)S(1)}, u32[]{:S(2)}, u32[]{:S(2)}) collective-permute-start(bf16[256,1024]{1,0:T(8,128)(2,1)S(1)} %get-tuple-element.24), channel_id=1, source_target_pairs={{0,4},{4,0},{8,12},{12,8},{1,5},{5,1},{9,13},{13,9},{2,6},{6,2},{1... | collective-permute-start | bytes 1572872 | tf_op jit(solution)/shard_map/ppermute | solution.py:319
  94.4 6.2 %collective-permute-start.6 = (bf16[256,1024]{1,0:T(8,128)(2,1)S(1)}, bf16[256,1024]{1,0:T(8,128)(2,1)S(1)}, u32[]{:S(2)}, u32[]{:S(2)}) collective-permute-start(bf16[256,1024]{1,0:T(8,128)(2,1)S(1)} %get-tuple-element.25), channel_id=1, source_target_pairs={{0,4},{4,0},{8,12},{12,8},{1,5},{5,1},{9,13},{13,9},{2,6},{6,2},{1... | collective-permute-start | bytes 1572872 | tf_op jit(solution)/shard_map/ppermute | solution.py:319
  95.0 48.3 %collective-permute-start.9 = (bf16[256,1024]{1,0:T(8,128)(2,1)S(1)}, bf16[256,1024]{1,0:T(8,128)(2,1)S(1)}, u32[]{:S(2)}, u32[]{:S(2)}) collective-permute-start(bf16[256,1024]{1,0:T(8,128)(2,1)S(1)} %back.7.refs_2_), channel_id=1, source_target_pairs={{0,8},{4,12},{8,0},{12,4},{1,9},{5,13},{9,1},{13,5},{2,10},{6,14},... | collective-permute-start | bytes 1572872 | tf_op jit(solution)/shard_map/ppermute | solution.py:316
  97.6 3.0 %copy-start.5 = (s32[32,32]{1,0:T(8,128)S(1)}, s32[32,32]{1,0:T(8,128)}, u32[]{:S(2)}) copy-start(s32[32,32]{1,0:T(8,128)} %refs_1_.5) | copy-start | bytes 12292
  120.0 1.0 copy-start.3
  121.1 29.3 %collective-permute-start.7 = (bf16[256,1024]{1,0:T(8,128)(2,1)S(1)}, bf16[256,1024]{1,0:T(8,128)(2,1)S(1)}, u32[]{:S(2)}, u32[]{:S(2)}) collective-permute-start(bf16[256,1024]{1,0:T(8,128)(2,1)S(1)} %relay.1.refs_1_), channel_id=1, source_target_pairs={{1,9},{2,1},{3,8},{5,13},{6,5},{7,12},{10,2},{9,10},{8,3},{14,6},{... | collective-permute-start | bytes 1572872 | tf_op jit(solution)/shard_map/ppermute | solution.py:328
  121.8 26.4 %collective-permute-start.8 = (bf16[256,512]{1,0:T(8,128)(2,1)S(1)}, bf16[256,512]{1,0:T(8,128)(2,1)S(1)}, u32[]{:S(2)}, u32[]{:S(2)}) collective-permute-start(bf16[256,512]{1,0:T(8,128)(2,1)S(1)} %back.8.refs_2_), channel_id=1, source_target_pairs={{0,8},{4,12},{8,0},{12,4},{1,9},{5,13},{9,1},{13,5},{2,10},{6,14},... | collective-permute-start | bytes 786440 | tf_op jit(solution)/shard_map/ppermute | solution.py:316
Sparse Core Ops, SparseCore 0:
  9.6 48.6 all-gather.1
  75.9 44.0 reduce-scatter.1
